TPU v7x, 128 devices: a whole 4x4x4 slice. The times are simulated.
128 devices in a mesh: gx: 8 (over z, core), gy: 16 (over x, y).
Axes of the slice: x: 4, y: 4, z: 4, core: 2. Of those that a mesh axis runs over, the one named last changes fastest.
Arguments:
- part_column: int32 [128, 128, 256], P(('gx', 'gy')), may hold values from 0 to 127
- part_layer: int32 [128, 128, 256], P(('gx', 'gy')), may hold values from 0 to 255
- part_count: int32 [128, 128], P(('gx', 'gy')), may hold values from 0 to 256, as said below
- part_data: float32 [128, 128, 7, 256], P(('gx', 'gy')), may hold values from -8 to 8, as said below
- source: float32 [128, 128, 256], P('gx', 'gy'), may hold values from -14 to 14
Outputs:
- porosity: float32 [128, 128, 256], P('gx', 'gy')
- drag_momentum_field: float32 [3, 128, 128, 256], P(None, 'gx', 'gy')
- pressure: float32 [128, 128, 256], P('gx', 'gy')
Inputs may be any that keep to these rules, and one draw needn't show every extreme that they name: `part_count`: slots of one source for one destination hold live particles first, then padding with arbitrary values; in every draw some destination device receives 256 particles from every source. `part_data`: rows 0 to 2 lie in [0, 1), row 3 is positive.
All inputs are finite; a program needn't handle non-finite values.
Results may differ from a plain program's by a relative error of at most 0.00013.
Values sent between devices are 32-bit elements; how exact they have to be, the bound alone decides.
A program may use at most 64 MiB of HBM per device.

v0:
```python
import math

import jax
import jax.numpy as jnp
from jax import lax
from jax.sharding import PartitionSpec as P

ITERS = 3


diag_shift = 0.01


def padded_2(block, sides, width):
    for axis, dim in sides:
        count = lax.axis_size(axis)
        forward = [(i, i + 1) for i in range(count - 1)]
        forward.append((count - 1, 0))
        backward = [(target, source) for source, target in forward]
        low = lax.ppermute(
            lax.slice_in_dim(block, block.shape[dim] - width, None, axis=dim), axis, forward
        )
        high = lax.ppermute(lax.slice_in_dim(block, 0, width, axis=dim), axis, backward)
        block = jnp.concatenate([low, block, high], axis=dim)
    return block


def shifted(block, axis, distance):
    devices = range(lax.axis_size(axis))
    route = [((i - distance) % len(devices), i) for i in devices]
    return lax.ppermute(block, axis, route)


def operate(values, stencil_weights):
    x_upper, x_lower, y_upper, y_lower, z_upper, z_lower = stencil_weights
    padded = padded_2(values, (("gx", 0), ("gy", 1)), 1)
    result = diag_shift * values
    result = result + x_upper * (values - padded[2:, 1:-1])
    result = result + x_lower * (values - padded[:-2, 1:-1])
    result = result + y_upper * (values - padded[1:-1, 2:])
    result = result + y_lower * (values - padded[1:-1, :-2])
    result = result + z_upper * (values - jnp.roll(values, -1, 2))
    result = result + z_lower * (values - jnp.roll(values, 1, 2))
    return result


def squares(former, latter):
    return lax.psum(jnp.sum(former * latter), ("gx", "gy"))


def curvature_sum(former, latter):
    return lax.psum(jnp.sum(former * latter), ("gx", "gy"))


def deposit_grid(
    cell_x, cell_y, layers, offset_x, offset_y, offset_z, loads, width_x, width_y, depth_z
):
    total_rows = cell_x.shape[0]
    block_rows = math.gcd(total_rows, 2048)
    block_count = total_rows // block_rows
    spots = (width_x + 1) * (width_y + 1)

    def split_rows(values):
        return values.reshape((block_count, block_rows) + values.shape[1:])

    def add_block(total, block):
        bx, by, bz, wox, woy, woz, bload = block
        spot_ids = lax.broadcasted_iota(jnp.int32, (block_rows, spots), 1)
        column_table = jnp.zeros((block_rows, spots), jnp.float32)
        for step_x in range(2):
            for step_y in range(2):
                weight_x = wox if step_x else 1.0 - wox
                weight_y = woy if step_y else 1.0 - woy
                target = (bx + step_x) * (width_y + 1) + by + step_y
                column_table = column_table + jnp.where(
                    target[:, None] == spot_ids, (weight_x * weight_y)[:, None], 0.0
                )
        layer_ids = lax.broadcasted_iota(jnp.int32, (block_rows, depth_z), 1)
        layer_table = jnp.where(bz[:, None] == layer_ids, (1.0 - woz)[:, None], 0.0)
        layer_table = layer_table + jnp.where(
            ((bz + 1) % depth_z)[:, None] == layer_ids, woz[:, None], 0.0
        )
        loaded = (bload[:, :, None] * layer_table[:, None, :]).reshape(block_rows, 4 * depth_z)
        product = lax.dot_general(
            column_table,
            loaded,
            (((0,), (0,)), ((), ())),
            precision=lax.Precision.HIGHEST,
            preferred_element_type=jnp.float32,
        )
        return (total + product, None)

    start = jnp.zeros((spots, 4 * depth_z), jnp.float32)
    blocks = tuple(
        (split_rows(v) for v in (cell_x, cell_y, layers, offset_x, offset_y, offset_z, loads))
    )
    total, unused = lax.scan(add_block, start, blocks)
    total = total.reshape(width_x + 1, width_y + 1, 4, depth_z)
    return jnp.moveaxis(total, 2, 0)


def shards(part_column, part_layer, part_count, part_data, source):
    columns = part_column[0]
    layers = part_layer[0]
    counts = part_count[0][:, None]
    payload = part_data[0]
    width_x, width_y, depth_z = source.shape
    columns, layers, payload, counts = (
        lax.all_to_all(columns, ("gx", "gy"), split_axis=0, concat_axis=0, tiled=True),
        lax.all_to_all(layers, ("gx", "gy"), split_axis=0, concat_axis=0, tiled=True),
        lax.all_to_all(payload, ("gx", "gy"), split_axis=0, concat_axis=0, tiled=True),
        lax.all_to_all(counts, ("gx", "gy"), split_axis=0, concat_axis=0, tiled=True),
    )
    slot_live = (lax.broadcasted_iota(jnp.int32, columns.shape, 1) < counts).astype(jnp.float32)
    cell_x = (columns // width_y).reshape(-1)
    cell_y = (columns % width_y).reshape(-1)
    loads = jnp.moveaxis(payload[:, 3:7] * slot_live[:, None, :], 1, 2).reshape(-1, 4)
    extended = deposit_grid(
        cell_x,
        cell_y,
        layers.reshape(-1),
        payload[:, 0].reshape(-1),
        payload[:, 1].reshape(-1),
        payload[:, 2].reshape(-1),
        loads,
        width_x,
        width_y,
        depth_z,
    )
    arriving = shifted(extended[:, width_x], "gx", 1)
    inner = extended[:, :width_x].at[:, 0].add(arriving)
    arriving = shifted(inner[:, :, width_y], "gy", 1)
    deposit = inner[:, :, :width_y].at[:, :, 0].add(arriving)
    porosity = 1.0 / (1.0 + deposit[0])
    drag_momentum_field = deposit[1:]
    stacked = jnp.stack([porosity, drag_momentum_field[0], drag_momentum_field[1]])
    halo_padded_grid = padded_2(stacked, (("gx", 1), ("gy", 2)), 1)
    divergence = 0.5 * (halo_padded_grid[1, 2:, 1:-1] - halo_padded_grid[1, :-2, 1:-1])
    divergence = divergence + 0.5 * (halo_padded_grid[2, 1:-1, 2:] - halo_padded_grid[2, 1:-1, :-2])
    divergence = divergence + 0.5 * (
        jnp.roll(drag_momentum_field[2], -1, 2) - jnp.roll(drag_momentum_field[2], 1, 2)
    )
    right_side = source - divergence
    border_porosity = halo_padded_grid[0]
    faces_along_xaxis = 0.5 * (border_porosity[:-1, 1:-1] + border_porosity[1:, 1:-1])
    faces_along_yaxis = 0.5 * (border_porosity[1:-1, :-1] + border_porosity[1:-1, 1:])
    x_upper = faces_along_xaxis[1:]
    x_lower = faces_along_xaxis[:-1]
    y_upper = faces_along_yaxis[:, 1:]
    y_lower = faces_along_yaxis[:, :-1]
    z_upper = 0.5 * (porosity + jnp.roll(porosity, -1, 2))
    z_lower = jnp.roll(z_upper, 1, 2)
    stencil_weights = (x_upper, x_lower, y_upper, y_lower, z_upper, z_lower)
    precond = 1.0 / (diag_shift + x_upper + x_lower + y_upper + y_lower + z_upper + z_lower)
    pressure = jnp.zeros_like(source)
    residual = right_side
    scaled = precond * residual
    direction = scaled
    product_now = squares(residual, scaled)
    for iteration in range(ITERS):
        applied = operate(direction, stencil_weights)
        step_size = product_now / curvature_sum(direction, applied)
        pressure = pressure + step_size * direction
        if iteration + 1 < ITERS:
            residual = residual - step_size * applied
            scaled = precond * residual
            product_next = squares(residual, scaled)
            direction = scaled + product_next / product_now * direction
            product_now = product_next
    return (porosity, drag_momentum_field, pressure)


def solution(mesh):
    placed = (
        P(("gx", "gy"), None, None),
        P(("gx", "gy"), None, None),
        P(("gx", "gy"), None),
        P(("gx", "gy"), None, None, None),
        P("gx", "gy", None),
    )
    return jax.shard_map(
        shards,
        mesh=mesh,
        in_specs=placed,
        out_specs=(P("gx", "gy", None), P(None, "gx", "gy", None), P("gx", "gy", None)),
        check_vma=False,
    )
```

profile of v0, /device:TPU:1, one launch (start us, length us, event | category | flops | bytes accessed | tf_op | source)
XLA Modules:
  0.0 917.3 jit_solution(5361567565905695540)
XLA Ops:
  2.0 11.5 %all-to-all-start.2 = ((s32[128,1,1]{2,1,0:T(1,128)}), s32[128,1,1]{2,1,0:T(1,128)S(1)}, u32[]{:S(2)}, u32[]{:S(2)}) async-start(s32[128,1,1]{2,1,0:T(1,128)} %copy.29), calls=%async_computation.2 | async-start | bytes 131072 | tf_op jit(solution)/shard_map/all_to_all | solution.py:112
  15.2 7.8 all-to-all-done.2
  29.2 8.4 all-to-all-done
  44.4 7.4 all-to-all-done.3
  59.2 15.4 %all-to-all-done.1 = f32[128,7,256]{2,1,0:T(8,128)S(1)} async-done(((f32[128,7,256]{2,1,0:T(8,128)}), f32[128,7,256]{2,1,0:T(8,128)S(1)}, u32[]{:S(2)}, u32[]{:S(2)}) %all-to-all-start.1) | async-done | bytes 917536 | tf_op jit(solution)/shard_map/all_to_all | solution.py:111
  76.6 446.5 %while.15 = (s32[]{:T(128)}, f32[153,1024]{1,0:T(8,128)}, s32[16,2048]{1,0:T(8,128)S(1)}, s32[16,2048]{1,0:T(8,128)S(1)}, f32[16,2048]{1,0:T(8,128)}, /*index=5*...) while((s32[]{:T(128)}, f32[153,1024]{1,0:T(8,128)}, ...), condition=%wide.region_1.2_spmd.clone, body=%wide.region_0.1_spmd.clone.sunk | while | flops 3858903040 | bytes 46817636 | solution.py:97
  92.5 12.0 %fusion.110 = f32[153,1024]{1,0:T(8,128)} fusion(f32[2048,1024]{1,0:T(8,128)} %bitcast.61, f32[2048]{0:T(1024)S(1)} %get-tuple-element.350, s32[2048]{0:T(1024)S(1)} %broadcast_add_fusion.4, f32[2048]{0:T(1024)S(1)} %get-tuple-element.352, s32[2048]{0:T(1024)S(1)} %bitcast.76, f32[2048]{0:T(1024)S(1)} %get-tuple-element.353, ...), kind=kOutput, calls=%fused_computation.16.clone.1 | convolution fusion | flops 3854131200 | bytes 9707521 | tf_op jit(solution)/shard_map/while/body/eval_jaxpr/dot_general | solution.py:84
  120.3 12.1 %fusion.110 = f32[153,1024]{1,0:T(8,128)} fusion(f32[2048,1024]{1,0:T(8,128)} %bitcast.61, f32[2048]{0:T(1024)S(1)} %get-tuple-element.350, s32[2048]{0:T(1024)S(1)} %broadcast_add_fusion.4, f32[2048]{0:T(1024)S(1)} %get-tuple-element.352, s32[2048]{0:T(1024)S(1)} %bitcast.76, f32[2048]{0:T(1024)S(1)} %get-tuple-element.353, ...), kind=kOutput, calls=%fused_computation.16.clone.1 | convolution fusion | flops 3854131200 | bytes 9707521 | tf_op jit(solution)/shard_map/while/body/eval_jaxpr/dot_general | solution.py:84
  148.2 12.1 %fusion.110 = f32[153,1024]{1,0:T(8,128)} fusion(f32[2048,1024]{1,0:T(8,128)} %bitcast.61, f32[2048]{0:T(1024)S(1)} %get-tuple-element.350, s32[2048]{0:T(1024)S(1)} %broadcast_add_fusion.4, f32[2048]{0:T(1024)S(1)} %get-tuple-element.352, s32[2048]{0:T(1024)S(1)} %bitcast.76, f32[2048]{0:T(1024)S(1)} %get-tuple-element.353, ...), kind=kOutput, calls=%fused_computation.16.clone.1 | convolution fusion | flops 3854131200 | bytes 9707521 | tf_op jit(solution)/shard_map/while/body/eval_jaxpr/dot_general | solution.py:84
  162.6 7.2 broadcast_multiply_fusion.2
  176.1 12.1 %fusion.110 = f32[153,1024]{1,0:T(8,128)} fusion(f32[2048,1024]{1,0:T(8,128)} %bitcast.61, f32[2048]{0:T(1024)S(1)} %get-tuple-element.350, s32[2048]{0:T(1024)S(1)} %broadcast_add_fusion.4, f32[2048]{0:T(1024)S(1)} %get-tuple-element.352, s32[2048]{0:T(1024)S(1)} %bitcast.76, f32[2048]{0:T(1024)S(1)} %get-tuple-element.353, ...), kind=kOutput, calls=%fused_computation.16.clone.1 | convolution fusion | flops 3854131200 | bytes 9707521 | tf_op jit(solution)/shard_map/while/body/eval_jaxpr/dot_general | solution.py:84
  204.0 12.1 %fusion.110 = f32[153,1024]{1,0:T(8,128)} fusion(f32[2048,1024]{1,0:T(8,128)} %bitcast.61, f32[2048]{0:T(1024)S(1)} %get-tuple-element.350, s32[2048]{0:T(1024)S(1)} %broadcast_add_fusion.4, f32[2048]{0:T(1024)S(1)} %get-tuple-element.352, s32[2048]{0:T(1024)S(1)} %bitcast.76, f32[2048]{0:T(1024)S(1)} %get-tuple-element.353, ...), kind=kOutput, calls=%fused_computation.16.clone.1 | convolution fusion | flops 3854131200 | bytes 9707521 | tf_op jit(solution)/shard_map/while/body/eval_jaxpr/dot_general | solution.py:84
  231.8 12.1 %fusion.110 = f32[153,1024]{1,0:T(8,128)} fusion(f32[2048,1024]{1,0:T(8,128)} %bitcast.61, f32[2048]{0:T(1024)S(1)} %get-tuple-element.350, s32[2048]{0:T(1024)S(1)} %broadcast_add_fusion.4, f32[2048]{0:T(1024)S(1)} %get-tuple-element.352, s32[2048]{0:T(1024)S(1)} %bitcast.76, f32[2048]{0:T(1024)S(1)} %get-tuple-element.353, ...), kind=kOutput, calls=%fused_computation.16.clone.1 | convolution fusion | flops 3854131200 | bytes 9707521 | tf_op jit(solution)/shard_map/while/body/eval_jaxpr/dot_general | solution.py:84
  259.7 12.1 %fusion.110 = f32[153,1024]{1,0:T(8,128)} fusion(f32[2048,1024]{1,0:T(8,128)} %bitcast.61, f32[2048]{0:T(1024)S(1)} %get-tuple-element.350, s32[2048]{0:T(1024)S(1)} %broadcast_add_fusion.4, f32[2048]{0:T(1024)S(1)} %get-tuple-element.352, s32[2048]{0:T(1024)S(1)} %bitcast.76, f32[2048]{0:T(1024)S(1)} %get-tuple-element.353, ...), kind=kOutput, calls=%fused_computation.16.clone.1 | convolution fusion | flops 3854131200 | bytes 9707521 | tf_op jit(solution)/shard_map/while/body/eval_jaxpr/dot_general | solution.py:84
  287.6 12.1 %fusion.110 = f32[153,1024]{1,0:T(8,128)} fusion(f32[2048,1024]{1,0:T(8,128)} %bitcast.61, f32[2048]{0:T(1024)S(1)} %get-tuple-element.350, s32[2048]{0:T(1024)S(1)} %broadcast_add_fusion.4, f32[2048]{0:T(1024)S(1)} %get-tuple-element.352, s32[2048]{0:T(1024)S(1)} %bitcast.76, f32[2048]{0:T(1024)S(1)} %get-tuple-element.353, ...), kind=kOutput, calls=%fused_computation.16.clone.1 | convolution fusion | flops 3854131200 | bytes 9707521 | tf_op jit(solution)/shard_map/while/body/eval_jaxpr/dot_general | solution.py:84
  302.1 7.2 broadcast_multiply_fusion.2
  315.5 12.1 %fusion.110 = f32[153,1024]{1,0:T(8,128)} fusion(f32[2048,1024]{1,0:T(8,128)} %bitcast.61, f32[2048]{0:T(1024)S(1)} %get-tuple-element.350, s32[2048]{0:T(1024)S(1)} %broadcast_add_fusion.4, f32[2048]{0:T(1024)S(1)} %get-tuple-element.352, s32[2048]{0:T(1024)S(1)} %bitcast.76, f32[2048]{0:T(1024)S(1)} %get-tuple-element.353, ...), kind=kOutput, calls=%fused_computation.16.clone.1 | convolution fusion | flops 3854131200 | bytes 9707521 | tf_op jit(solution)/shard_map/while/body/eval_jaxpr/dot_general | solution.py:84
  343.4 12.1 %fusion.110 = f32[153,1024]{1,0:T(8,128)} fusion(f32[2048,1024]{1,0:T(8,128)} %bitcast.61, f32[2048]{0:T(1024)S(1)} %get-tuple-element.350, s32[2048]{0:T(1024)S(1)} %broadcast_add_fusion.4, f32[2048]{0:T(1024)S(1)} %get-tuple-element.352, s32[2048]{0:T(1024)S(1)} %bitcast.76, f32[2048]{0:T(1024)S(1)} %get-tuple-element.353, ...), kind=kOutput, calls=%fused_computation.16.clone.1 | convolution fusion | flops 3854131200 | bytes 9707521 | tf_op jit(solution)/shard_map/while/body/eval_jaxpr/dot_general | solution.py:84
  357.8 7.2 broadcast_multiply_fusion.2
  371.3 12.1 %fusion.110 = f32[153,1024]{1,0:T(8,128)} fusion(f32[2048,1024]{1,0:T(8,128)} %bitcast.61, f32[2048]{0:T(1024)S(1)} %get-tuple-element.350, s32[2048]{0:T(1024)S(1)} %broadcast_add_fusion.4, f32[2048]{0:T(1024)S(1)} %get-tuple-element.352, s32[2048]{0:T(1024)S(1)} %bitcast.76, f32[2048]{0:T(1024)S(1)} %get-tuple-element.353, ...), kind=kOutput, calls=%fused_computation.16.clone.1 | convolution fusion | flops 3854131200 | bytes 9707521 | tf_op jit(solution)/shard_map/while/body/eval_jaxpr/dot_general | solution.py:84
  385.7 7.2 broadcast_multiply_fusion.2
  399.2 12.1 %fusion.110 = f32[153,1024]{1,0:T(8,128)} fusion(f32[2048,1024]{1,0:T(8,128)} %bitcast.61, f32[2048]{0:T(1024)S(1)} %get-tuple-element.350, s32[2048]{0:T(1024)S(1)} %broadcast_add_fusion.4, f32[2048]{0:T(1024)S(1)} %get-tuple-element.352, s32[2048]{0:T(1024)S(1)} %bitcast.76, f32[2048]{0:T(1024)S(1)} %get-tuple-element.353, ...), kind=kOutput, calls=%fused_computation.16.clone.1 | convolution fusion | flops 3854131200 | bytes 9707521 | tf_op jit(solution)/shard_map/while/body/eval_jaxpr/dot_general | solution.py:84
  427.0 12.1 %fusion.110 = f32[153,1024]{1,0:T(8,128)} fusion(f32[2048,1024]{1,0:T(8,128)} %bitcast.61, f32[2048]{0:T(1024)S(1)} %get-tuple-element.350, s32[2048]{0:T(1024)S(1)} %broadcast_add_fusion.4, f32[2048]{0:T(1024)S(1)} %get-tuple-element.352, s32[2048]{0:T(1024)S(1)} %bitcast.76, f32[2048]{0:T(1024)S(1)} %get-tuple-element.353, ...), kind=kOutput, calls=%fused_computation.16.clone.1 | convolution fusion | flops 3854131200 | bytes 9707521 | tf_op jit(solution)/shard_map/while/body/eval_jaxpr/dot_general | solution.py:84
  441.5 7.2 broadcast_multiply_fusion.2
  454.9 12.1 %fusion.110 = f32[153,1024]{1,0:T(8,128)} fusion(f32[2048,1024]{1,0:T(8,128)} %bitcast.61, f32[2048]{0:T(1024)S(1)} %get-tuple-element.350, s32[2048]{0:T(1024)S(1)} %broadcast_add_fusion.4, f32[2048]{0:T(1024)S(1)} %get-tuple-element.352, s32[2048]{0:T(1024)S(1)} %bitcast.76, f32[2048]{0:T(1024)S(1)} %get-tuple-element.353, ...), kind=kOutput, calls=%fused_computation.16.clone.1 | convolution fusion | flops 3854131200 | bytes 9707521 | tf_op jit(solution)/shard_map/while/body/eval_jaxpr/dot_general | solution.py:84
  482.8 12.1 %fusion.110 = f32[153,1024]{1,0:T(8,128)} fusion(f32[2048,1024]{1,0:T(8,128)} %bitcast.61, f32[2048]{0:T(1024)S(1)} %get-tuple-element.350, s32[2048]{0:T(1024)S(1)} %broadcast_add_fusion.4, f32[2048]{0:T(1024)S(1)} %get-tuple-element.352, s32[2048]{0:T(1024)S(1)} %bitcast.76, f32[2048]{0:T(1024)S(1)} %get-tuple-element.353, ...), kind=kOutput, calls=%fused_computation.16.clone.1 | convolution fusion | flops 3854131200 | bytes 9707521 | tf_op jit(solution)/shard_map/while/body/eval_jaxpr/dot_general | solution.py:84
  510.7 12.1 %fusion.110 = f32[153,1024]{1,0:T(8,128)} fusion(f32[2048,1024]{1,0:T(8,128)} %bitcast.61, f32[2048]{0:T(1024)S(1)} %get-tuple-element.350, s32[2048]{0:T(1024)S(1)} %broadcast_add_fusion.4, f32[2048]{0:T(1024)S(1)} %get-tuple-element.352, s32[2048]{0:T(1024)S(1)} %bitcast.76, f32[2048]{0:T(1024)S(1)} %get-tuple-element.353, ...), kind=kOutput, calls=%fused_computation.16.clone.1 | convolution fusion | flops 3854131200 | bytes 9707521 | tf_op jit(solution)/shard_map/while/body/eval_jaxpr/dot_general | solution.py:84
  561.8 65.7 %all-reduce = (f32[]{:T(128)}, f32[]{:T(128)}) all-reduce(f32[]{:T(128)} %get-tuple-element.203, f32[]{:T(128)} %get-tuple-element.202), channel_id=1, replica_groups=mesh['gx'=8,'gy'=16] {'gx','gy'}, use_global_device_ids=true, to_apply=%region_3.4 | all-reduce | flops 2 | bytes 16 | tf_op jit(solution)/shard_map/psum | solution.py:48
  629.5 62.5 %psum.44 = f32[]{:T(128)} all-reduce(f32[]{:T(128)} %get-tuple-element.226), channel_id=1, replica_groups=mesh['gx'=8,'gy'=16] {'gx','gy'}, use_global_device_ids=true, to_apply=%region_7.8 | all-reduce | flops 1 | bytes 8 | tf_op jit(solution)/shard_map/psum | solution.py:48
  705.6 65.4 %psum.45 = f32[]{:T(128)} all-reduce(f32[]{:T(128)} %get-tuple-element.224), channel_id=1, replica_groups=mesh['gx'=8,'gy'=16] {'gx','gy'}, use_global_device_ids=true, to_apply=%region_9.10 | all-reduce | flops 1 | bytes 8 | tf_op jit(solution)/shard_map/psum | solution.py:52
  773.0 62.5 %psum.46 = f32[]{:T(128)} all-reduce(f32[]{:T(128)} %multiply_reduce_fusion), channel_id=1, replica_groups=mesh['gx'=8,'gy'=16] {'gx','gy'}, use_global_device_ids=true, to_apply=%region_11.12 | all-reduce | flops 1 | bytes 8 | tf_op jit(solution)/shard_map/psum | solution.py:48
  849.8 65.4 %psum.47 = f32[]{:T(128)} all-reduce(f32[]{:T(128)} %fusion.31), channel_id=1, replica_groups=mesh['gx'=8,'gy'=16] {'gx','gy'}, use_global_device_ids=true, to_apply=%region_13.14 | all-reduce | flops 1 | bytes 8 | tf_op jit(solution)/shard_map/psum | solution.py:52
  (565 shorter events, 304.5 us)
Async XLA Ops:
  2.0 21.0 %all-to-all-start.2 = ((s32[128,1,1]{2,1,0:T(1,128)}), s32[128,1,1]{2,1,0:T(1,128)S(1)}, u32[]{:S(2)}, u32[]{:S(2)}) async-start(s32[128,1,1]{2,1,0:T(1,128)} %copy.29), calls=%async_computation.2 | async-start | bytes 131072 | tf_op jit(solution)/shard_map/all_to_all | solution.py:112
  23.0 14.6 %all-to-all-start = ((s32[128,1,256]{2,1,0:T(1,128)}), s32[128,1,256]{2,1,0:T(1,128)S(1)}, u32[]{:S(2)}, u32[]{:S(2)}) async-start(s32[128,1,256]{2,1,0:T(1,128)} %all_to_all.23), calls=%async_computation | async-start | bytes 262144 | tf_op jit(solution)/shard_map/all_to_all | solution.py:109
  37.6 14.2 %all-to-all-start.3 = ((s32[128,1,256]{2,1,0:T(1,128)}), s32[128,1,256]{2,1,0:T(1,128)S(1)}, u32[]{:S(2)}, u32[]{:S(2)}) async-start(s32[128,1,256]{2,1,0:T(1,128)} %all_to_all.29), calls=%async_computation.3 | async-start | bytes 262144 | tf_op jit(solution)/shard_map/all_to_all | solution.py:110
  51.8 22.8 %all-to-all-start.1 = ((f32[128,7,256]{2,1,0:T(8,128)}), f32[128,7,256]{2,1,0:T(8,128)S(1)}, u32[]{:S(2)}, u32[]{:S(2)}) async-start(f32[128,7,256]{2,1,0:T(8,128)} %bitcast.38), calls=%async_computation.1 | async-start | bytes 2097152 | tf_op jit(solution)/shard_map/all_to_all | solution.py:111
  120.3 12.2 %copy-start.2 = (f32[16,2048,4]{1,2,0:T(4,128)S(1)}, f32[16,2048,4]{1,2,0:T(4,128)}, u32[]{:S(2)}) copy-start(f32[16,2048,4]{1,2,0:T(4,128)} %copy-done.1) | copy-start | bytes 1572868 | tf_op jit(solution)/shard_map/while
  148.1 12.2 %copy-start.2 = (f32[16,2048,4]{1,2,0:T(4,128)S(1)}, f32[16,2048,4]{1,2,0:T(4,128)}, u32[]{:S(2)}) copy-start(f32[16,2048,4]{1,2,0:T(4,128)} %copy-done.1) | copy-start | bytes 1572868 | tf_op jit(solution)/shard_map/while
  176.0 12.2 %copy-start.2 = (f32[16,2048,4]{1,2,0:T(4,128)S(1)}, f32[16,2048,4]{1,2,0:T(4,128)}, u32[]{:S(2)}) copy-start(f32[16,2048,4]{1,2,0:T(4,128)} %copy-done.1) | copy-start | bytes 1572868 | tf_op jit(solution)/shard_map/while
  203.9 12.2 %copy-start.2 = (f32[16,2048,4]{1,2,0:T(4,128)S(1)}, f32[16,2048,4]{1,2,0:T(4,128)}, u32[]{:S(2)}) copy-start(f32[16,2048,4]{1,2,0:T(4,128)} %copy-done.1) | copy-start | bytes 1572868 | tf_op jit(solution)/shard_map/while
  231.8 12.2 %copy-start.2 = (f32[16,2048,4]{1,2,0:T(4,128)S(1)}, f32[16,2048,4]{1,2,0:T(4,128)}, u32[]{:S(2)}) copy-start(f32[16,2048,4]{1,2,0:T(4,128)} %copy-done.1) | copy-start | bytes 1572868 | tf_op jit(solution)/shard_map/while
  287.6 12.2 %copy-start.2 = (f32[16,2048,4]{1,2,0:T(4,128)S(1)}, f32[16,2048,4]{1,2,0:T(4,128)}, u32[]{:S(2)}) copy-start(f32[16,2048,4]{1,2,0:T(4,128)} %copy-done.1) | copy-start | bytes 1572868 | tf_op jit(solution)/shard_map/while
  371.2 12.2 %copy-start.2 = (f32[16,2048,4]{1,2,0:T(4,128)S(1)}, f32[16,2048,4]{1,2,0:T(4,128)}, u32[]{:S(2)}) copy-start(f32[16,2048,4]{1,2,0:T(4,128)} %copy-done.1) | copy-start | bytes 1572868 | tf_op jit(solution)/shard_map/while
  454.9 12.2 %copy-start.2 = (f32[16,2048,4]{1,2,0:T(4,128)S(1)}, f32[16,2048,4]{1,2,0:T(4,128)}, u32[]{:S(2)}) copy-start(f32[16,2048,4]{1,2,0:T(4,128)} %copy-done.1) | copy-start | bytes 1572868 | tf_op jit(solution)/shard_map/while
  524.4 3.0 collective-permute-start
  529.2 6.5 collective-permute-start.1
  536.7 12.3 %copy-start = (f32[16,8,256]{2,1,0:T(8,128)}, f32[16,8,256]{2,1,0:T(8,128)S(1)}, u32[]{:S(2)}) copy-start(f32[16,8,256]{2,1,0:T(8,128)S(1)} %get-tuple-element.247) | copy-start | bytes 393220
  536.8 12.2 %copy-start.9 = (f32[16,8,256]{2,1,0:T(8,128)S(1)}, f32[16,8,256]{2,1,0:T(8,128)}, u32[]{:S(2)}) copy-start(f32[16,8,256]{2,1,0:T(8,128)} %param.15) | copy-start | bytes 393220
  536.8 5.1 collective-permute-start.2
  541.1 1.2 collective-permute-start.3
  542.4 3.1 collective-permute-start.4
  542.4 6.4 collective-permute-start.5
  549.2 5.3 collective-permute-start.6
  553.7 1.2 collective-permute-start.7
  554.9 2.7 collective-permute-start.8
  554.9 6.0 collective-permute-start.9
  693.4 3.1 collective-permute-start.10
  694.0 2.6 collective-permute-start.11
  696.6 3.1 collective-permute-start.12
  698.8 5.9 collective-permute-start.13
  836.9 3.1 collective-permute-start.14
  837.5 2.6 collective-permute-start.15
  840.1 3.1 collective-permute-start.16
  842.3 5.9 collective-permute-start.17
  (120 other events, 742.8 us)
where the time goes:
time: 919 us; the launch traced here: 917 us
  blocking collectives  322 us (35%)
  matrix products  194 us (21%)
  other arithmetic  143 us (16%)
  local copies, waits for them, and re-layouts  130 us (14%)
  waiting for transfers between devices  71.3 us (8%)
  starting transfers between devices  46.5 us (5%)
    dot_general x16, matrix products, add_block(): lax.dot_general(column_table, loaded, (((0,), (0,)), ((), ())), precision...  194 us
    psum x3, blocking collectives, squares(): return lax.psum(jnp.sum(former * latter), ('gx', 'gy'))  191 us
    psum x2, blocking collectives, curvature_sum(): return lax.psum(jnp.sum(former * latter), ('gx', 'gy'))  131 us
    mul x16, other arithmetic, add_block(): bload[:, :, None] * layer_table[:, None, :]  115 us
    while x272, local copies, waits for them, and re-layouts  95 us
  transfers between devices with their start and end apart: 22, of which 22 were waited for; matrix products, arithmetic and copies ran while one was open for 1% of the time, Pallas kernels for 0%

commit v1 on v0

v1 whole, which is shorter than its diff:
```python
import jax
import jax.numpy as jnp
from jax import lax
from jax.experimental import pallas as pl
from jax.experimental.pallas import tpu as pltpu
from jax.sharding import PartitionSpec as P

diag_shift = 0.01
WX, WY, NZ, CAP = 16, 8, 256, 256
NGX, NGY = 8, 16
MAIN = (WX + 1) * 4 * WY
ROWS = MAIN + 80
VALUES = 9
f32, bf16 = jnp.float32, jnp.bfloat16
MESH = pl.DeviceIdType.MESH


def split(a):
    high = a.astype(bf16)
    return high, (a - high.astype(f32)).astype(bf16)


def tables(row):
    part = [row[:, CAP * i : CAP * (i + 1)] for i in range(VALUES)]
    column, bz = part[0].astype(jnp.int32), part[1].astype(jnp.int32)
    ox, oy, oz = part[2:5]
    bx, by = column >> 3, column & 7
    xi = lax.broadcasted_iota(jnp.int32, (72, CAP), 0) >> 2
    fi = lax.broadcasted_iota(jnp.int32, (8, CAP), 0) & 3
    loads = jnp.where(fi == 0, part[5], jnp.where(fi == 1, part[6], jnp.where(fi == 2, part[7], part[8])))
    wx = jnp.where(bx == xi, 1.0 - ox, jnp.where(bx + 1 == xi, ox, 0.0))
    xf = (wx.reshape(9, 8, CAP) * loads[None]).reshape(72, CAP)
    yi = lax.broadcasted_iota(jnp.int32, (8, CAP), 0)
    wy = jnp.where(by == yi, 1.0 - oy, jnp.where(by + 1 == yi, oy, 0.0))
    over = jnp.where(by == 7, oy, 0.0)
    main = (xf[:68, None, :] * wy[None]).reshape(MAIN, CAP)
    extra = jnp.concatenate([xf * over, jnp.zeros((8, CAP), f32)], 0)
    q = jnp.round(oz * 256.0) * (1.0 / 256.0)
    e = oz - q
    zi = lax.broadcasted_iota(jnp.int32, (NZ, CAP), 0)
    here, above = zi == bz, zi == ((bz + 1) & (NZ - 1))
    z_high = jnp.where(here, 1.0 - q, jnp.where(above, q, 0.0)).astype(bf16)
    z_low = jnp.where(here, -e, jnp.where(above, e, 0.0)).astype(bf16)
    return split(main), split(extra), (z_high, z_low)


def dot_nt(a, b):
    return lax.dot_general(a, b, (((1,), (1,)), ((), ())), preferred_element_type=f32)


GROUP = 8


def deposit_kernel(parts_ref, total_ref):
    total_ref[...] = jnp.zeros_like(total_ref)

    def step(i, carry):
        main, extra, layer = [], [], []
        for g in range(GROUP):
            (mh, ml), (eh, el), (zh, zl) = tables(parts_ref[i * GROUP + g])
            main += [mh, ml, mh]
            extra += [eh, el, eh]
            layer += [zh, zh, zl]
        right = jnp.concatenate(layer, 1)
        total_ref[:MAIN] += dot_nt(jnp.concatenate(main, 1), right)
        total_ref[MAIN:] += dot_nt(jnp.concatenate(extra, 1), right)
        return carry

    lax.fori_loop(0, parts_ref.shape[0] // GROUP, step, 0)


def deposit(parts):
    return pl.pallas_call(
        deposit_kernel,
        out_shape=jax.ShapeDtypeStruct((ROWS, NZ), f32),
        in_specs=[pl.BlockSpec(memory_space=pltpu.VMEM)],
        out_specs=pl.BlockSpec(memory_space=pltpu.VMEM),
        compiler_params=pltpu.CompilerParams(vmem_limit_bytes=48 << 20),
        name="deposit",
    )(parts)


def tail_kernel(
    total, source, porosity_out, drag_out, pressure_out,
    over_x, over_y, over_c, poro, face, y_send, y_recv, u0, u1, u2, red, red_x, red_y,
    over_send, over_recv, halo_send, halo_recv, rx_send, rx_recv, ry_send, ry_recv,
):
    gx, gy = lax.axis_index("gx"), lax.axis_index("gy")
    xp, xm = lax.rem(gx + 1, NGX), lax.rem(gx + NGX - 1, NGX)
    yp, ym = lax.rem(gy + 1, NGY), lax.rem(gy + NGY - 1, NGY)
    barrier = pltpu.get_barrier_semaphore()
    for k in range(1, NGX):
        pl.semaphore_signal(barrier, inc=1, device_id=(lax.rem(gx + k, NGX), gy), device_id_type=MESH)
    for k in range(1, NGY):
        pl.semaphore_signal(barrier, inc=1, device_id=(gx, lax.rem(gy + k, NGY)), device_id_type=MESH)
    pl.semaphore_signal(barrier, inc=1, device_id=(xp, yp), device_id_type=MESH)
    pl.semaphore_signal(barrier, inc=1, device_id=(xm, ym), device_id_type=MESH)
    pl.semaphore_wait(barrier, NGX + NGY)

    def send(src, dst, send_sem, recv_sem, to):
        copy = pltpu.make_async_remote_copy(
            src_ref=src, dst_ref=dst, send_sem=send_sem, recv_sem=recv_sem, device_id=to, device_id_type=MESH
        )
        copy.start()
        return copy

    copies = [
        send(total.at[pl.ds(512, 32)], over_x, over_send.at[0], over_recv.at[0], (xp, gy)),
        send(total.at[pl.ds(MAIN, 64)], over_y, over_send.at[1], over_recv.at[1], (gx, yp)),
        send(total.at[pl.ds(MAIN + 64, 8)], over_c, over_send.at[2], over_recv.at[2], (xp, yp)),
    ]
    for copy in copies:
        copy.wait()
    from_y = jnp.concatenate([over_y[:8] + over_c[...], over_y[8:]], 0)
    inner = total[:512].reshape(64, 8, NZ)
    inner = jnp.concatenate([inner[:4] + over_x[...].reshape(4, 8, NZ), inner[4:]], 0)
    row = lax.broadcasted_iota(jnp.int32, (64, 8, NZ), 1)
    inner = inner + jnp.where(row == 0, from_y[:, None, :], 0.0)
    inner = inner.reshape(WX, 4, 8, NZ)
    porosity = 1.0 / (1.0 + inner[:, 0])
    drag = [inner[:, 1], inner[:, 2], inner[:, 3]]
    porosity_out[...] = porosity
    for m in range(3):
        drag_out[m] = drag[m]

    poro[0, 1 : WX + 1] = porosity
    poro[1, 1 : WX + 1] = drag[0]

    def exchange(k, fields, y_faces):
        n = y_faces[0].shape[0]
        y_send[k, 0, :n] = y_faces[0]
        y_send[k, 1, :n] = y_faces[1]
        copies = [
            send(fields(WX), fields(0), halo_send.at[k, 0], halo_recv.at[k, 0], (xp, gy)),
            send(fields(1), fields(WX + 1), halo_send.at[k, 1], halo_recv.at[k, 1], (xm, gy)),
            send(y_send.at[k, 0, pl.ds(0, n)], y_recv.at[k, 0, pl.ds(0, n)], halo_send.at[k, 2], halo_recv.at[k, 2], (gx, yp)),
            send(y_send.at[k, 1, pl.ds(0, n)], y_recv.at[k, 1, pl.ds(0, n)], halo_send.at[k, 3], halo_recv.at[k, 3], (gx, ym)),
        ]
        for copy in copies:
            copy.wait()

    def y_faces(values):
        return tuple(jnp.stack([v[:, y] for v in values]) for y in (7, 0))

    exchange(0, lambda x: poro.at[pl.ds(0, 2), x], y_faces([porosity, drag[1]]))

    yi = lax.broadcasted_iota(jnp.int32, (WX, 8, NZ), 1)

    def y_next(v, k, i):
        return jnp.where(yi == 7, y_recv[k, 1, i][:, None, :], pltpu.roll(v, 7, 1))

    def y_previous(v, k, i):
        return jnp.where(yi == 0, y_recv[k, 0, i][:, None, :], pltpu.roll(v, 1, 1))

    def z_next(v):
        return pltpu.roll(v, NZ - 1, 2)

    def z_previous(v):
        return pltpu.roll(v, 1, 2)

    divergence = 0.5 * (poro[1, 2:] - poro[1, :WX])
    divergence = divergence + 0.5 * (y_next(drag[1], 0, 1) - y_previous(drag[1], 0, 1))
    divergence = divergence + 0.5 * (z_next(drag[2]) - z_previous(drag[2]))
    right_side = source[...] - divergence
    x_upper = 0.5 * (porosity + poro[0, 2:])
    x_lower = 0.5 * (poro[0, :WX] + porosity)
    y_upper = 0.5 * (porosity + y_next(porosity, 0, 0))
    y_lower = 0.5 * (y_previous(porosity, 0, 0) + porosity)
    z_upper = 0.5 * (porosity + z_next(porosity))
    z_lower = z_previous(z_upper)
    precond = 1.0 / (diag_shift + x_upper + x_lower + y_upper + y_lower + z_upper + z_lower)
    for i, weights in enumerate((x_upper, x_lower, y_upper, y_lower, z_upper, z_lower, precond)):
        face[i] = weights

    def operate(k, u):
        v = u[1 : WX + 1]
        exchange(k, lambda x: u.at[x], tuple(v[:, y][None] for y in (7, 0)))
        result = diag_shift * v
        result = result + face[0] * (v - u[2:])
        result = result + face[1] * (v - u[:WX])
        result = result + face[2] * (v - y_next(v, k, 0))
        result = result + face[3] * (v - y_previous(v, k, 0))
        result = result + face[4] * (v - z_next(v))
        result = result + face[5] * (v - z_previous(v))
        return v, result

    def partial_sum(a, b):
        product = jnp.sum(a * b, 0)
        return jnp.sum(product[:, :128] + product[:, 128:], 0, keepdims=True)

    start = precond * right_side
    u0[1 : WX + 1] = start
    moments = [partial_sum(right_side, start)]
    v0, a0 = operate(1, u0)
    v1 = face[6] * a0
    u1[1 : WX + 1] = v1
    moments += [partial_sum(v0, a0), partial_sum(v1, a0)]
    v1, a1 = operate(2, u1)
    v2 = face[6] * a1
    u2[1 : WX + 1] = v2
    moments += [partial_sum(v1, a1), partial_sum(v2, a1)]
    v2, a2 = operate(3, u2)
    moments += [partial_sum(v2, a2)]

    zero = jnp.zeros((2, 128), f32)
    mine = jnp.concatenate(moments + [zero], 0)
    red[0] = mine
    red_x[gx] = mine
    copies = [
        send(red.at[0], red_x.at[gx], rx_send.at[k], rx_recv.at[k], (lax.rem(gx + k, NGX), gy)) for k in range(1, NGX)
    ]
    for copy in copies:
        copy.wait()
    mine = jnp.sum(red_x[...], 0)
    red[1] = mine
    red_y[gy] = mine
    copies = [
        send(red.at[1], red_y.at[gy], ry_send.at[k], ry_recv.at[k], (gx, lax.rem(gy + k, NGY))) for k in range(1, NGY)
    ]
    for copy in copies:
        copy.wait()
    sums = jnp.sum(jnp.sum(red_y[...], 0), 1, keepdims=True)
    m0, m1, m2, m3, m4, m5 = [sums[i : i + 1] for i in range(6)]
    l21, l31 = m2 / m1, m3 / m1
    d2 = m3 - l21 * m2
    e32 = m4 - l31 * m2
    r1 = m1 - l21 * m0
    r2 = m2 - l31 * m0
    l32 = e32 / d2
    d3 = (m5 - l31 * m3) - l32 * e32
    c2 = (r2 - l32 * r1) / d3
    c1 = r1 / d2 - l32 * c2
    c0 = m0 / m1 - l21 * c1 - l31 * c2
    c0, c1, c2 = [c.reshape(1, 1, 1) for c in (c0, c1, c2)]
    pressure_out[...] = c0 * u0[1 : WX + 1] + c1 * u1[1 : WX + 1] + c2 * u2[1 : WX + 1]


def tail(total, source):
    vmem = pl.BlockSpec(memory_space=pltpu.VMEM)
    block = (WX, WY, NZ)
    padded = (WX + 2, WY, NZ)
    dma = pltpu.SemaphoreType.DMA
    return pl.pallas_call(
        tail_kernel,
        out_shape=(
            jax.ShapeDtypeStruct(block, f32),
            jax.ShapeDtypeStruct((3,) + block, f32),
            jax.ShapeDtypeStruct(block, f32),
        ),
        in_specs=[vmem, vmem],
        out_specs=(vmem, vmem, vmem),
        scratch_shapes=[
            pltpu.VMEM((32, NZ), f32),
            pltpu.VMEM((64, NZ), f32),
            pltpu.VMEM((8, NZ), f32),
            pltpu.VMEM((2,) + padded, f32),
            pltpu.VMEM((7,) + block, f32),
            pltpu.VMEM((4, 2, 2, WX, NZ), f32),
            pltpu.VMEM((4, 2, 2, WX, NZ), f32),
            pltpu.VMEM(padded, f32),
            pltpu.VMEM(padded, f32),
            pltpu.VMEM(padded, f32),
            pltpu.VMEM((2, 8, 128), f32),
            pltpu.VMEM((NGX, 8, 128), f32),
            pltpu.VMEM((NGY, 8, 128), f32),
            dma((3,)), dma((3,)), dma((4, 4)), dma((4, 4)),
            dma((NGX,)), dma((NGX,)), dma((NGY,)), dma((NGY,)),
        ],
        compiler_params=pltpu.CompilerParams(
            collective_id=0, has_side_effects=True, vmem_limit_bytes=48 << 20
        ),
        name="tail",
    )(total, source)


def shards(part_column, part_layer, part_count, part_data, source):
    live = lax.broadcasted_iota(jnp.int32, (1, 1, CAP), 2) < part_count[0][:, None, None]
    data = part_data[0]
    packed = jnp.concatenate(
        [
            part_column[0].astype(f32)[:, None],
            part_layer[0].astype(f32)[:, None],
            data[:, :3],
            jnp.where(live, data[:, 3:], 0.0),
        ],
        axis=1,
    ).reshape(-1, 1, VALUES * CAP)
    parts = lax.all_to_all(packed, ("gx", "gy"), split_axis=0, concat_axis=0, tiled=True)
    return tail(deposit(parts), source)


def solution(mesh):
    placed = (
        P(("gx", "gy"), None, None),
        P(("gx", "gy"), None, None),
        P(("gx", "gy"), None),
        P(("gx", "gy"), None, None, None),
        P("gx", "gy", None),
    )
    return jax.shard_map(
        shards,
        mesh=mesh,
        in_specs=placed,
        out_specs=(P("gx", "gy", None), P(None, "gx", "gy", None), P("gx", "gy", None)),
        check_vma=False,
    )
```

time: 919 us -> 126 us (0.14)
  blocking collectives: 322 us -> 31.2 us
  matrix products: 194 us -> 0 us
  other arithmetic: 143 us -> 0.83 us
  local copies, waits for them, and re-layouts: 130 us -> 7.17 us
  Pallas kernels: 0 us -> 85.7 us
  waiting for transfers between devices: 71.3 us -> 0 us
  starting transfers between devices: 46.5 us -> 0 us
    psum x5 -> x0, blocking collectives: 322 us -> none  [the longest x3 191 us: squares(): return lax.psum(jnp.sum(former * latter), ('gx', 'gy'))]
    dot_general x16 -> x0, matrix products: 194 us -> none  [add_block(): lax.dot_general(column_table, loaded, (((0,), (0,)), ((), ())), precision...]
    mul x37 -> x0, other arithmetic: 116 us -> none  [the longest x16 115 us: add_block(): bload[:, :, None] * layer_table[:, None, :]]
    while x272 -> x0, local copies, waits for them, and re-layouts: 95 us -> none
    pallas_call x0 -> x2, Pallas kernels: none -> 85.7 us  [the longest x1 50.4 us: deposit(): pl.pallas_call(deposit_kernel, out_shape=jax.ShapeDtypeStruct((ROWS, NZ),...]
    all_to_all x4 -> x0, waiting for transfers between devices: 39.1 us -> none  [the longest x1 15.4 us: shards(): lax.all_to_all(payload, ('gx', 'gy'), split_axis=0, concat_axis=0, tiled=...]
    ppermute x18 -> x0, waiting for transfers between devices: 32.2 us -> none  [the longest x8 17.7 us: padded_2(): lax.ppermute(lax.slice_in_dim(block, block.shape[dim] - width, None, axis...]
    all_to_all x0 -> x1, blocking collectives: none -> 31.2 us  [shards(): lax.all_to_all(packed, ('gx', 'gy'), split_axis=0, concat_axis=0, tiled=T...]
  transfers between devices with their start and end apart: 22 -> 0, of which waited for: 22 -> 0; matrix products, arithmetic and copies ran while one was open for 1% -> 0% of each run, Pallas kernels for 0% -> 0%
where the time goes in v1:
time: 126 us
  Pallas kernels  85.7 us (68%)
  blocking collectives  31.2 us (25%)
  local copies, waits for them, and re-layouts  7.17 us (6%)
    pallas_call x1, Pallas kernels, deposit(): pl.pallas_call(deposit_kernel, out_shape=jax.ShapeDtypeStruct((ROWS, NZ),...  50.4 us
    pallas_call x1, Pallas kernels, tail(): pl.pallas_call(tail_kernel, out_shape=(jax.ShapeDtypeStruct(block, f32),...  35.3 us
    all_to_all x1, blocking collectives, shards(): lax.all_to_all(packed, ('gx', 'gy'), split_axis=0, concat_axis=0, tiled=T...  31.2 us
    unnamed x8, local copies, waits for them, and re-layouts  5.53 us

profile of v1, /device:TPU:1, one launch (start us, length us, event | category | flops | bytes accessed | tf_op | source)
XLA Modules:
  0.0 125.7 jit_solution(11399490178125170723)
XLA Ops:
  0.6 0.7 iota_compare_fusion
  1.3 1.0 copy.9
  2.3 1.0 copy.10
  3.3 1.5 %copy.11 = f32[1,128,7,256]{1,3,2,0:T(8,128)S(1)} copy(f32[1,128,7,256]{3,1,2,0:T(8,128)} %param.8) | data formatting | bytes 1835008 | tf_op args[3]
  4.9 0.1 pad_maximum_fusion
  5.0 1.6 %copy.12 = f32[128,1,2304]{2,1,0:T(1,128)S(1)} copy(f32[128,1,2304]{0,2,1:T(8,128)S(1)} %bitcast.7) | data formatting | bytes 2359296 | tf_op jit(solution)/shard_map/reshape | solution.py:287
  6.6 31.2 %all_to_all.5.parts_ref = f32[128,1,2304]{2,1,0:T(1,128)S(1)} all-to-all(f32[128,1,2304]{2,1,0:T(1,128)S(1)} %copy.12), channel_id=1, replica_groups=mesh['gx'=8,'gy'=16] {'gx','gy'}, dimensions={0} | all-to-all | bytes 2359296 | tf_op jit(solution)/shard_map/all_to_all | solution.py:288
  37.9 0.0 copy-start
  37.9 50.4 %deposit.1.total = f32[624,256]{1,0:T(8,128)S(1)} custom-call(f32[128,1,2304]{2,1,0:T(1,128)S(1)} %all_to_all.5.parts_ref), custom_call_target="tpu_custom_call" | custom-call | tf_op jit(solution)/shard_map/deposit/pallas_call | solution.py:73
  88.3 0.0 copy-done
  88.3 35.3 %tail.1 = (f32[16,8,256]{2,1,0:T(8,128)S(1)}, f32[3,16,8,256]{3,2,1,0:T(8,128)S(1)}, f32[16,8,256]{2,1,0:T(8,128)S(1)}) custom-call(f32[624,256]{1,0:T(8,128)S(1)} %deposit.1.total, f32[16,8,256]{2,1,0:T(8,128)S(1)} %copy-done), custom_call_target="tpu_custom_call" | custom-call | tf_op jit(solution)/shard_map/tail/pallas_call | solution.py:243
  123.6 0.7 copy.16
  124.3 0.7 copy.17
  125.0 0.7 copy.18
  (3 shorter events, 0.1 us)
Async XLA Ops:
  37.9 50.4 %copy-start = (f32[16,8,256]{2,1,0:T(8,128)S(1)}, f32[16,8,256]{2,1,0:T(8,128)}, u32[]{:S(2)}) copy-start(f32[16,8,256]{2,1,0:T(8,128)} %source.1) | copy-start | bytes 393220

commit v2 on v1

--- a/solution.py
+++ b/solution.py
@@ -15,87 +15,122 @@
 MESH = pl.DeviceIdType.MESH
 
 
-def split(a):
-    high = a.astype(bf16)
-    return high, (a - high.astype(f32)).astype(bf16)
-
-
-def tables(row):
-    part = [row[:, CAP * i : CAP * (i + 1)] for i in range(VALUES)]
-    column, bz = part[0].astype(jnp.int32), part[1].astype(jnp.int32)
-    ox, oy, oz = part[2:5]
+def tables(slot, k):
+    part = [slot[k, i : i + 1] for i in range(VALUES)]
+    ox, oy, oz = part[:3]
+    column, bz = part[7].astype(jnp.int32), part[8].astype(jnp.int32)
     bx, by = column >> 3, column & 7
     xi = lax.broadcasted_iota(jnp.int32, (72, CAP), 0) >> 2
     fi = lax.broadcasted_iota(jnp.int32, (8, CAP), 0) & 3
-    loads = jnp.where(fi == 0, part[5], jnp.where(fi == 1, part[6], jnp.where(fi == 2, part[7], part[8])))
+    loads = jnp.where(fi == 0, part[3], jnp.where(fi == 1, part[4], jnp.where(fi == 2, part[5], part[6])))
     wx = jnp.where(bx == xi, 1.0 - ox, jnp.where(bx + 1 == xi, ox, 0.0))
     xf = (wx.reshape(9, 8, CAP) * loads[None]).reshape(72, CAP)
     yi = lax.broadcasted_iota(jnp.int32, (8, CAP), 0)
     wy = jnp.where(by == yi, 1.0 - oy, jnp.where(by + 1 == yi, oy, 0.0))
     over = jnp.where(by == 7, oy, 0.0)
     main = (xf[:68, None, :] * wy[None]).reshape(MAIN, CAP)
-    extra = jnp.concatenate([xf * over, jnp.zeros((8, CAP), f32)], 0)
+    left = jnp.concatenate([main, xf * over, jnp.zeros((8, CAP), f32)], 0)
+    high = left.astype(bf16)
+    low = (left - high.astype(f32)).astype(bf16)
     q = jnp.round(oz * 256.0) * (1.0 / 256.0)
     e = oz - q
     zi = lax.broadcasted_iota(jnp.int32, (NZ, CAP), 0)
     here, above = zi == bz, zi == ((bz + 1) & (NZ - 1))
     z_high = jnp.where(here, 1.0 - q, jnp.where(above, q, 0.0)).astype(bf16)
     z_low = jnp.where(here, -e, jnp.where(above, e, 0.0)).astype(bf16)
-    return split(main), split(extra), (z_high, z_low)
+    return high, low, z_high, z_low
 
 
 def dot_nt(a, b):
     return lax.dot_general(a, b, (((1,), (1,)), ((), ())), preferred_element_type=f32)
 
 
-GROUP = 8
-
-
-def deposit_kernel(parts_ref, total_ref):
-    total_ref[...] = jnp.zeros_like(total_ref)
-
-    def step(i, carry):
-        main, extra, layer = [], [], []
-        for g in range(GROUP):
-            (mh, ml), (eh, el), (zh, zl) = tables(parts_ref[i * GROUP + g])
-            main += [mh, ml, mh]
-            extra += [eh, el, eh]
-            layer += [zh, zh, zl]
-        right = jnp.concatenate(layer, 1)
-        total_ref[:MAIN] += dot_nt(jnp.concatenate(main, 1), right)
-        total_ref[MAIN:] += dot_nt(jnp.concatenate(extra, 1), right)
-        return carry
-
-    lax.fori_loop(0, parts_ref.shape[0] // GROUP, step, 0)
-
-
-def deposit(parts):
-    return pl.pallas_call(
-        deposit_kernel,
-        out_shape=jax.ShapeDtypeStruct((ROWS, NZ), f32),
-        in_specs=[pl.BlockSpec(memory_space=pltpu.VMEM)],
-        out_specs=pl.BlockSpec(memory_space=pltpu.VMEM),
-        compiler_params=pltpu.CompilerParams(vmem_limit_bytes=48 << 20),
-        name="deposit",
-    )(parts)
-
-
-def tail_kernel(
-    total, source, porosity_out, drag_out, pressure_out,
+GROUP = 16
+DEVICES = NGX * NGY
+
+
+def kernel(
+    counts, columns, layers, data, source, porosity_out, drag_out, pressure_out,
+    packed, slots, total, all_send, all_recv,
     over_x, over_y, over_c, poro, face, y_send, y_recv, u0, u1, u2, red, red_x, red_y,
     over_send, over_recv, halo_send, halo_recv, rx_send, rx_recv, ry_send, ry_recv,
 ):
     gx, gy = lax.axis_index("gx"), lax.axis_index("gy")
     xp, xm = lax.rem(gx + 1, NGX), lax.rem(gx + NGX - 1, NGX)
     yp, ym = lax.rem(gy + 1, NGY), lax.rem(gy + NGY - 1, NGY)
+
+    def peer(k):
+        return lax.rem(gx + lax.rem(k, NGX), NGX), lax.rem(gy + lax.div(k, NGX), NGY)
+
     barrier = pltpu.get_barrier_semaphore()
-    for k in range(1, NGX):
-        pl.semaphore_signal(barrier, inc=1, device_id=(lax.rem(gx + k, NGX), gy), device_id_type=MESH)
-    for k in range(1, NGY):
-        pl.semaphore_signal(barrier, inc=1, device_id=(gx, lax.rem(gy + k, NGY)), device_id_type=MESH)
-    pl.semaphore_signal(barrier, inc=1, device_id=(xp, yp), device_id_type=MESH)
-    pl.semaphore_signal(barrier, inc=1, device_id=(xm, ym), device_id_type=MESH)
-    pl.semaphore_wait(barrier, NGX + NGY)
+
+    def greet(k, carry):
+        pl.semaphore_signal(barrier, inc=1, device_id=peer(k), device_id_type=MESH)
+        return carry
+
+    lax.fori_loop(1, DEVICES, greet, 0)
+
+    lane = lax.broadcasted_iota(jnp.int32, (8, CAP), 1)
+    row = lax.broadcasted_iota(jnp.int32, (8, CAP), 0)
+
+    def pack(d):
+        live = lane < counts[0, d]
+        values = jnp.concatenate([data[d], columns[pl.ds(d, 1)].astype(f32)], 0)
+        return jnp.where(live | (row < 3) | (row == 7), values, 0.0), layers[pl.ds(d, 1)].astype(f32)
+
+    own = gx * NGY + gy
+    upper, lower = pack(own)
+    slots[0, :8] = upper
+    slots[0, 8:] = lower
+
+    pl.semaphore_wait(barrier, DEVICES - 1)
+
+    def ship(k, carry):
+        px, py = peer(k)
+        upper, lower = pack(px * NGY + py)
+        packed[k, :8] = upper
+        packed[k, 8:] = lower
+        pltpu.make_async_remote_copy(
+            src_ref=packed.at[k],
+            dst_ref=slots.at[k],
+            send_sem=all_send,
+            recv_sem=all_recv.at[lax.div(k, GROUP)],
+            device_id=(px, py),
+            device_id_type=MESH,
+        ).start()
+        return carry
+
+    lax.fori_loop(1, DEVICES, ship, 0)
+
+    def arrived(group, first, count):
+        block = slots.at[pl.ds(first, count)]
+        pltpu.make_async_copy(block, block, all_recv.at[group]).wait()
+
+    def add_group(i):
+        left, right = [], []
+        for g in range(GROUP):
+            high, low, z_high, z_low = tables(slots, i * GROUP + g)
+            left += [high, low, high]
+            right += [z_high, z_high, z_low]
+        return dot_nt(jnp.concatenate(left, 1), jnp.concatenate(right, 1))
+
+    total[...] = jnp.zeros_like(total)
+
+    def step(i, carry):
+        @pl.when(i == 0)
+        def _():
+            arrived(0, 1, GROUP - 1)
+
+        @pl.when(i > 0)
+        def _():
+            arrived(i, i * GROUP, GROUP)
+
+        total[...] += add_group(i)
+        return carry
+
+    lax.fori_loop(0, DEVICES // GROUP, step, 0)
+    shipped = packed.at[pl.ds(1, DEVICES - 1)]
+    pltpu.make_async_copy(shipped, shipped, all_send).wait()
 
     def send(src, dst, send_sem, recv_sem, to):
         copy = pltpu.make_async_remote_copy(
@@ -235,21 +270,25 @@
     pressure_out[...] = c0 * u0[1 : WX + 1] + c1 * u1[1 : WX + 1] + c2 * u2[1 : WX + 1]
 
 
-def tail(total, source):
+def run(counts, columns, layers, data, source):
     vmem = pl.BlockSpec(memory_space=pltpu.VMEM)
     block = (WX, WY, NZ)
     padded = (WX + 2, WY, NZ)
     dma = pltpu.SemaphoreType.DMA
     return pl.pallas_call(
-        tail_kernel,
+        kernel,
         out_shape=(
             jax.ShapeDtypeStruct(block, f32),
             jax.ShapeDtypeStruct((3,) + block, f32),
             jax.ShapeDtypeStruct(block, f32),
         ),
-        in_specs=[vmem, vmem],
+        in_specs=[pl.BlockSpec(memory_space=pltpu.SMEM), vmem, vmem, vmem, vmem],
         out_specs=(vmem, vmem, vmem),
         scratch_shapes=[
+            pltpu.VMEM((DEVICES, VALUES, CAP), f32),
+            pltpu.VMEM((DEVICES, VALUES, CAP), f32),
+            pltpu.VMEM((ROWS, NZ), f32),
+            dma(()), dma((DEVICES // GROUP,)),
             pltpu.VMEM((32, NZ), f32),
             pltpu.VMEM((64, NZ), f32),
             pltpu.VMEM((8, NZ), f32),
@@ -269,24 +308,12 @@
         compiler_params=pltpu.CompilerParams(
             collective_id=0, has_side_effects=True, vmem_limit_bytes=48 << 20
         ),
-        name="tail",
-    )(total, source)
+        name="coupling",
+    )(counts, columns, layers, data, source)
 
 
 def shards(part_column, part_layer, part_count, part_data, source):
-    live = lax.broadcasted_iota(jnp.int32, (1, 1, CAP), 2) < part_count[0][:, None, None]
-    data = part_data[0]
-    packed = jnp.concatenate(
-        [
-            part_column[0].astype(f32)[:, None],
-            part_layer[0].astype(f32)[:, None],
-            data[:, :3],
-            jnp.where(live, data[:, 3:], 0.0),
-        ],
-        axis=1,
-    ).reshape(-1, 1, VALUES * CAP)
-    parts = lax.all_to_all(packed, ("gx", "gy"), split_axis=0, concat_axis=0, tiled=True)
-    return tail(deposit(parts), source)
+    return run(part_count, part_column[0], part_layer[0], part_data[0], source)
 
 
 def solution(mesh):

time: 126 us -> 115 us (0.913)
  blocking collectives: 31.2 us -> 0 us
  Pallas kernels: 85.7 us -> 109 us
  local copies, waits for them, and re-layouts: 7.17 us -> 4.46 us
    all_to_all x1 -> x0, blocking collectives: 31.2 us -> none  [shards(): lax.all_to_all(packed, ('gx', 'gy'), split_axis=0, concat_axis=0, tiled=T...]
    pallas_call x2 -> x1, Pallas kernels: 85.7 us -> 109 us  [run(): pl.pallas_call(kernel, out_shape=(jax.ShapeDtypeStruct(block, f32), jax.S...]
    reshape x1 -> x0, local copies, waits for them, and re-layouts: 1.61 us -> none  [shards(): packed = jnp.concatenate([part_column[0].astype(f32)[:, None], part_layer...]
    unnamed x8 -> x12, local copies, waits for them, and re-layouts: 5.53 us -> 4.46 us
where the time goes in v2:
time: 115 us; the launch traced here: 114 us
  Pallas kernels  109 us (95%)
  local copies, waits for them, and re-layouts  4.46 us (4%)
    pallas_call x1, Pallas kernels, run(): pl.pallas_call(kernel, out_shape=(jax.ShapeDtypeStruct(block, f32), jax.S...  109 us
    unnamed x12, local copies, waits for them, and re-layouts  4.46 us

profile of v2, /device:TPU:1, one launch (start us, length us, event | category | flops | bytes accessed | tf_op | source)
XLA Modules:
  0.0 114.4 jit_solution(11031856859094793828)
XLA Ops:
  0.6 0.0 copy-start
  0.6 0.0 copy-start.1
  0.7 0.0 copy-start.2
  0.7 1.8 %copy.10 = f32[1,128,7,256]{3,2,1,0:T(8,128)S(1)} copy(f32[1,128,7,256]{3,1,2,0:T(8,128)} %param.8) | data formatting | bytes 1835008 | tf_op args[3]
  2.4 0.0 copy-start.3
  2.4 0.0 copy-done
  2.5 0.0 copy-done.1
  2.5 0.0 copy-done.2
  2.5 0.6 copy-done.3
  3.1 109.2 %coupling.1 = (f32[16,8,256]{2,1,0:T(8,128)S(1)}, f32[3,16,8,256]{3,2,1,0:T(8,128)S(1)}, f32[16,8,256]{2,1,0:T(8,128)S(1)}) custom-call(s32[1,128]{1,0:T(1,128)S(1)} %copy-done.3, s32[128,256]{1,0:T(8,128)S(1)} %bitcast.6, s32[128,256]{1,0:T(8,128)S(1)} %bitcast.7, f32[128,7,256]{2,1,0:T(8,128)S(1)} %bitcast.5, f32[16,8,256]{2,1,0:T(8,128)S(1)} %copy-done.2), custom_call_target="tpu_custom_call" | custom-call | tf_op jit(solution)/shard_map/coupling/pallas_call | solution.py:278
  112.3 0.7 copy.14
  113.0 0.7 copy.15
  113.7 0.7 copy.16
Async XLA Ops:
  0.6 1.8 %copy-start = (s32[1,128,256]{2,1,0:T(8,128)S(1)}, s32[1,128,256]{2,1,0:T(8,128)}, u32[]{:S(2)}) copy-start(s32[1,128,256]{2,1,0:T(8,128)} %param.5) | copy-start | bytes 393220
  0.6 1.8 %copy-start.1 = (s32[1,128,256]{2,1,0:T(8,128)S(1)}, s32[1,128,256]{2,1,0:T(8,128)}, u32[]{:S(2)}) copy-start(s32[1,128,256]{2,1,0:T(8,128)} %param.6) | copy-start | bytes 393220
  0.7 1.8 %copy-start.2 = (f32[16,8,256]{2,1,0:T(8,128)S(1)}, f32[16,8,256]{2,1,0:T(8,128)}, u32[]{:S(2)}) copy-start(f32[16,8,256]{2,1,0:T(8,128)} %source.1) | copy-start | bytes 393220
  2.4 0.7 copy-start.3

commit v3 on v2

--- a/solution.py
+++ b/solution.py
@@ -16,7 +16,7 @@
 
 
 def tables(slot, k):
-    part = [slot[k, i : i + 1] for i in range(VALUES)]
+    part = [slot[k, :, CAP * i : CAP * (i + 1)] for i in range(VALUES)]
     ox, oy, oz = part[:3]
     column, bz = part[7].astype(jnp.int32), part[8].astype(jnp.int32)
     bx, by = column >> 3, column & 7
@@ -45,7 +45,8 @@
     return lax.dot_general(a, b, (((1,), (1,)), ((), ())), preferred_element_type=f32)
 
 
-GROUP = 16
+GROUP = 8
+AHEAD = 4
 DEVICES = NGX * NGY
 
 
@@ -64,43 +65,42 @@
 
     barrier = pltpu.get_barrier_semaphore()
 
+    lane = lax.broadcasted_iota(jnp.int32, (1, CAP), 1)
+
+    def pack(target, k, d):
+        live = lane < counts[0, d]
+        rows = data[d]
+        for i in range(7):
+            row = rows[i : i + 1]
+            target[k, :, CAP * i : CAP * (i + 1)] = row if i < 3 else jnp.where(live, row, 0.0)
+        target[k, :, CAP * 7 : CAP * 8] = columns[pl.ds(d, 1)].astype(f32)
+        target[k, :, CAP * 8 :] = layers[pl.ds(d, 1)].astype(f32)
+
     def greet(k, carry):
-        pl.semaphore_signal(barrier, inc=1, device_id=peer(k), device_id_type=MESH)
+        px, py = peer(k)
+        pl.semaphore_signal(barrier, inc=1, device_id=(px, py), device_id_type=MESH)
+        pack(packed, k, px * NGY + py)
         return carry
 
     lax.fori_loop(1, DEVICES, greet, 0)
-
-    lane = lax.broadcasted_iota(jnp.int32, (8, CAP), 1)
-    row = lax.broadcasted_iota(jnp.int32, (8, CAP), 0)
-
-    def pack(d):
-        live = lane < counts[0, d]
-        values = jnp.concatenate([data[d], columns[pl.ds(d, 1)].astype(f32)], 0)
-        return jnp.where(live | (row < 3) | (row == 7), values, 0.0), layers[pl.ds(d, 1)].astype(f32)
-
-    own = gx * NGY + gy
-    upper, lower = pack(own)
-    slots[0, :8] = upper
-    slots[0, 8:] = lower
-
+    pack(slots, 0, gx * NGY + gy)
     pl.semaphore_wait(barrier, DEVICES - 1)
 
-    def ship(k, carry):
-        px, py = peer(k)
-        upper, lower = pack(px * NGY + py)
-        packed[k, :8] = upper
-        packed[k, 8:] = lower
+    def ship(group, g):
+        k = group * GROUP + g
         pltpu.make_async_remote_copy(
             src_ref=packed.at[k],
             dst_ref=slots.at[k],
             send_sem=all_send,
-            recv_sem=all_recv.at[lax.div(k, GROUP)],
-            device_id=(px, py),
+            recv_sem=all_recv.at[group],
+            device_id=peer(k),
             device_id_type=MESH,
         ).start()
-        return carry
-
-    lax.fori_loop(1, DEVICES, ship, 0)
+
+    for group in range(AHEAD):
+        for g in range(GROUP):
+            if group + g > 0:
+                ship(group, g)
 
     def arrived(group, first, count):
         block = slots.at[pl.ds(first, count)]
@@ -116,7 +116,7 @@
 
     total[...] = jnp.zeros_like(total)
 
-    def step(i, carry):
+    def step(i, shipping):
         @pl.when(i == 0)
         def _():
             arrived(0, 1, GROUP - 1)
@@ -125,10 +125,14 @@
         def _():
             arrived(i, i * GROUP, GROUP)
 
+        if shipping:
+            for g in range(GROUP):
+                ship(i + AHEAD, g)
         total[...] += add_group(i)
-        return carry
-
-    lax.fori_loop(0, DEVICES // GROUP, step, 0)
+
+    groups = DEVICES // GROUP
+    lax.fori_loop(0, groups - AHEAD, lambda i, c: (step(i, True), c)[1], 0)
+    lax.fori_loop(groups - AHEAD, groups, lambda i, c: (step(i, False), c)[1], 0)
     shipped = packed.at[pl.ds(1, DEVICES - 1)]
     pltpu.make_async_copy(shipped, shipped, all_send).wait()
 
@@ -285,8 +289,8 @@
         in_specs=[pl.BlockSpec(memory_space=pltpu.SMEM), vmem, vmem, vmem, vmem],
         out_specs=(vmem, vmem, vmem),
         scratch_shapes=[
-            pltpu.VMEM((DEVICES, VALUES, CAP), f32),
-            pltpu.VMEM((DEVICES, VALUES, CAP), f32),
+            pltpu.VMEM((DEVICES, 1, VALUES * CAP), f32),
+            pltpu.VMEM((DEVICES, 1, VALUES * CAP), f32),
             pltpu.VMEM((ROWS, NZ), f32),
             dma(()), dma((DEVICES // GROUP,)),
             pltpu.VMEM((32, NZ), f32),

time: 115 us -> 95 us (0.83)
  Pallas kernels: 109 us -> 89.7 us
    pallas_call x1, Pallas kernels: 109 us -> 89.7 us  [run(): pl.pallas_call(kernel, out_shape=(jax.ShapeDtypeStruct(block, f32), jax.S...]
where the time goes in v3:
time: 95 us; the launch traced here: 94.9 us
  Pallas kernels  89.7 us (94%)
  local copies, waits for them, and re-layouts  4.46 us (5%)
    pallas_call x1, Pallas kernels, run(): pl.pallas_call(kernel, out_shape=(jax.ShapeDtypeStruct(block, f32), jax.S...  89.7 us
    unnamed x12, local copies, waits for them, and re-layouts  4.46 us

profile of v3, /device:TPU:1, one launch (start us, length us, event | category | flops | bytes accessed | tf_op | source)
XLA Modules:
  0.0 94.9 jit_solution(3882390747276625438)
XLA Ops:
  0.6 0.0 copy-start
  0.6 0.0 copy-start.1
  0.7 0.0 copy-start.2
  0.7 1.8 %copy.10 = f32[1,128,7,256]{3,2,1,0:T(8,128)S(1)} copy(f32[1,128,7,256]{3,1,2,0:T(8,128)} %param.8) | data formatting | bytes 1835008 | tf_op args[3]
  2.4 0.0 copy-start.3
  2.4 0.0 copy-done
  2.5 0.0 copy-done.1
  2.5 0.0 copy-done.2
  2.5 0.6 copy-done.3
  3.1 89.7 %coupling.1 = (f32[16,8,256]{2,1,0:T(8,128)S(1)}, f32[3,16,8,256]{3,2,1,0:T(8,128)S(1)}, f32[16,8,256]{2,1,0:T(8,128)S(1)}) custom-call(s32[1,128]{1,0:T(1,128)S(1)} %copy-done.3, s32[128,256]{1,0:T(8,128)S(1)} %bitcast.6, s32[128,256]{1,0:T(8,128)S(1)} %bitcast.7, f32[128,7,256]{2,1,0:T(8,128)S(1)} %bitcast.5, f32[16,8,256]{2,1,0:T(8,128)S(1)} %copy-done.2), custom_call_target="tpu_custom_call" | custom-call | tf_op jit(solution)/shard_map/coupling/pallas_call | solution.py:282
  92.8 0.7 copy.14
  93.5 0.7 copy.15
  94.2 0.7 copy.16
Async XLA Ops:
  0.6 1.8 %copy-start = (s32[1,128,256]{2,1,0:T(8,128)S(1)}, s32[1,128,256]{2,1,0:T(8,128)}, u32[]{:S(2)}) copy-start(s32[1,128,256]{2,1,0:T(8,128)} %param.5) | copy-start | bytes 393220
  0.6 1.8 %copy-start.1 = (s32[1,128,256]{2,1,0:T(8,128)S(1)}, s32[1,128,256]{2,1,0:T(8,128)}, u32[]{:S(2)}) copy-start(s32[1,128,256]{2,1,0:T(8,128)} %param.6) | copy-start | bytes 393220
  0.7 1.8 %copy-start.2 = (f32[16,8,256]{2,1,0:T(8,128)S(1)}, f32[16,8,256]{2,1,0:T(8,128)}, u32[]{:S(2)}) copy-start(f32[16,8,256]{2,1,0:T(8,128)} %source.1) | copy-start | bytes 393220
  2.4 0.7 copy-start.3

commit v4 on v3

--- a/solution.py
+++ b/solution.py
@@ -18,7 +18,7 @@
 def tables(slot, k):
     part = [slot[k, :, CAP * i : CAP * (i + 1)] for i in range(VALUES)]
     ox, oy, oz = part[:3]
-    column, bz = part[7].astype(jnp.int32), part[8].astype(jnp.int32)
+    column = part[7].astype(jnp.int32)
     bx, by = column >> 3, column & 7
     xi = lax.broadcasted_iota(jnp.int32, (72, CAP), 0) >> 2
     fi = lax.broadcasted_iota(jnp.int32, (8, CAP), 0) & 3
@@ -34,10 +34,13 @@
     low = (left - high.astype(f32)).astype(bf16)
     q = jnp.round(oz * 256.0) * (1.0 / 256.0)
     e = oz - q
-    zi = lax.broadcasted_iota(jnp.int32, (NZ, CAP), 0)
-    here, above = zi == bz, zi == ((bz + 1) & (NZ - 1))
-    z_high = jnp.where(here, 1.0 - q, jnp.where(above, q, 0.0)).astype(bf16)
-    z_low = jnp.where(here, -e, jnp.where(above, e, 0.0)).astype(bf16)
+    zi = lax.broadcasted_iota(jnp.int32, (NZ, CAP), 0).astype(f32).astype(bf16)
+    here = zi == part[8].astype(bf16)
+    above = zi == jnp.where(part[8] == NZ - 1.0, 0.0, part[8] + 1.0).astype(bf16)
+    zero = jnp.zeros((), bf16)
+    rest = e.astype(bf16)
+    z_high = jnp.where(here, (1.0 - q).astype(bf16), jnp.where(above, q.astype(bf16), zero))
+    z_low = jnp.where(here, -rest, jnp.where(above, rest, zero))
     return high, low, z_high, z_low
 
 
@@ -46,6 +49,8 @@
 
 
 GROUP = 8
+HALO = 3
+WIDE = WX + 2 * HALO
 AHEAD = 4
 DEVICES = NGX * NGY
 
@@ -53,8 +58,8 @@
 def kernel(
     counts, columns, layers, data, source, porosity_out, drag_out, pressure_out,
     packed, slots, total, all_send, all_recv,
-    over_x, over_y, over_c, poro, face, y_send, y_recv, u0, u1, u2, red, red_x, red_y,
-    over_send, over_recv, halo_send, halo_recv, rx_send, rx_recv, ry_send, ry_recv,
+    over_x, over_y, over_c, dx_face, dy_send, dy_recv, y_send, y_recv, corner, face, poro, u0, u1, u2,
+    red, red_x, red_y, over_send, over_recv, dx_send, dx_recv, halo_send, halo_recv, rx_send, rx_recv, ry_send, ry_recv,
 ):
     gx, gy = lax.axis_index("gx"), lax.axis_index("gy")
     xp, xm = lax.rem(gx + 1, NGX), lax.rem(gx + NGX - 1, NGX)
@@ -77,12 +82,19 @@
         target[k, :, CAP * 8 :] = layers[pl.ds(d, 1)].astype(f32)
 
     def greet(k, carry):
+        pl.semaphore_signal(barrier, inc=1, device_id=peer(k), device_id_type=MESH)
+        return carry
+
+    def pack_one(k, carry):
         px, py = peer(k)
-        pl.semaphore_signal(barrier, inc=1, device_id=(px, py), device_id_type=MESH)
         pack(packed, k, px * NGY + py)
         return carry
 
-    lax.fori_loop(1, DEVICES, greet, 0)
+    def greet_and_pack(k, carry):
+        return pack_one(k, greet(k, carry))
+
+    lax.fori_loop(1, AHEAD * GROUP, greet_and_pack, 0)
+    lax.fori_loop(AHEAD * GROUP, DEVICES, greet, 0)
     pack(slots, 0, gx * NGY + gy)
     pl.semaphore_wait(barrier, DEVICES - 1)
 
@@ -127,6 +139,7 @@
 
         if shipping:
             for g in range(GROUP):
+                pack_one((i + AHEAD) * GROUP + g, 0)
                 ship(i + AHEAD, g)
         total[...] += add_group(i)
 
@@ -162,34 +175,59 @@
     for m in range(3):
         drag_out[m] = drag[m]
 
-    poro[0, 1 : WX + 1] = porosity
-    poro[1, 1 : WX + 1] = drag[0]
-
-    def exchange(k, fields, y_faces):
-        n = y_faces[0].shape[0]
-        y_send[k, 0, :n] = y_faces[0]
-        y_send[k, 1, :n] = y_faces[1]
-        copies = [
-            send(fields(WX), fields(0), halo_send.at[k, 0], halo_recv.at[k, 0], (xp, gy)),
-            send(fields(1), fields(WX + 1), halo_send.at[k, 1], halo_recv.at[k, 1], (xm, gy)),
-            send(y_send.at[k, 0, pl.ds(0, n)], y_recv.at[k, 0, pl.ds(0, n)], halo_send.at[k, 2], halo_recv.at[k, 2], (gx, yp)),
-            send(y_send.at[k, 1, pl.ds(0, n)], y_recv.at[k, 1, pl.ds(0, n)], halo_send.at[k, 3], halo_recv.at[k, 3], (gx, ym)),
+    own_x, own_y = pl.ds(HALO, WX), pl.ds(8, 8)
+
+    def send_halo(k, ref):
+        pair = ref[own_x, own_y].reshape(WX // 2, 2, 8, NZ)
+        even, odd = pair[:, 0], pair[:, 1]
+        upper_half = lax.broadcasted_iota(jnp.int32, (WX // 2, 8, NZ), 1) >= 4
+        y_send[k, 0] = jnp.where(upper_half, odd, pltpu.roll(even, 4, 1))
+        y_send[k, 1] = jnp.where(upper_half, pltpu.roll(odd, 4, 1), even)
+        last = WX // 2 - 1
+
+        def put(i, src, dst, to):
+            return send(src, dst, halo_send.at[k, i], halo_recv.at[k, i], to)
+
+        return [
+            put(0, y_send.at[k, 0], y_recv.at[k, 0], (gx, yp)),
+            put(1, y_send.at[k, 1], y_recv.at[k, 1], (gx, ym)),
+            put(2, ref.at[pl.ds(WX, HALO), own_y], ref.at[pl.ds(0, HALO), own_y], (xp, gy)),
+            put(3, ref.at[pl.ds(HALO, HALO), own_y], ref.at[pl.ds(WX + HALO, HALO), own_y], (xm, gy)),
+            put(4, y_send.at[k, 0, last], corner.at[k, 0], (xp, yp)),
+            put(5, y_send.at[k, 1, last], corner.at[k, 1], (xp, ym)),
+            put(6, y_send.at[k, 0, 0], corner.at[k, 2], (xm, yp)),
+            put(7, y_send.at[k, 1, 0], corner.at[k, 3], (xm, ym)),
         ]
-        for copy in copies:
-            copy.wait()
-
-    def y_faces(values):
-        return tuple(jnp.stack([v[:, y] for v in values]) for y in (7, 0))
-
-    exchange(0, lambda x: poro.at[pl.ds(0, 2), x], y_faces([porosity, drag[1]]))
+
+    def place_faces(k, ref):
+        low, high = y_recv[k, 0], y_recv[k, 1]
+        ref[own_x, :8] = jnp.stack([pltpu.roll(low, 4, 1), low], 1).reshape(WX, 8, NZ)
+        ref[own_x, 16:] = jnp.stack([high, pltpu.roll(high, 4, 1)], 1).reshape(WX, 8, NZ)
+
+    def place_corners(k, ref):
+        for i, x in ((0, 1), (2, WX + HALO)):
+            low, high = corner[k, i], corner[k, i + 1]
+            ref[x, :8] = pltpu.roll(low, 4, 0)
+            ref[x + 1, :8] = low
+            ref[x, 16:] = high
+            ref[x + 1, 16:] = pltpu.roll(high, 4, 0)
+
+    poro[own_x, own_y] = porosity
+    dx_face[1 : WX + 1] = drag[0]
+    dy_send[0] = drag[1][:, 7]
+    dy_send[1] = drag[1][:, 0]
+    drags = [
+        send(dy_send.at[0], dy_recv.at[0], dx_send.at[0], dx_recv.at[0], (gx, yp)),
+        send(dy_send.at[1], dy_recv.at[1], dx_send.at[1], dx_recv.at[1], (gx, ym)),
+        send(dx_face.at[WX], dx_face.at[0], dx_send.at[2], dx_recv.at[2], (xp, gy)),
+        send(dx_face.at[1], dx_face.at[WX + 1], dx_send.at[3], dx_recv.at[3], (xm, gy)),
+    ]
+    halo = send_halo(0, poro)
+    for copy in drags + halo[:4]:
+        copy.wait()
+    place_faces(0, poro)
 
     yi = lax.broadcasted_iota(jnp.int32, (WX, 8, NZ), 1)
-
-    def y_next(v, k, i):
-        return jnp.where(yi == 7, y_recv[k, 1, i][:, None, :], pltpu.roll(v, 7, 1))
-
-    def y_previous(v, k, i):
-        return jnp.where(yi == 0, y_recv[k, 0, i][:, None, :], pltpu.roll(v, 1, 1))
 
     def z_next(v):
         return pltpu.roll(v, NZ - 1, 2)
@@ -197,49 +235,78 @@
     def z_previous(v):
         return pltpu.roll(v, 1, 2)
 
-    divergence = 0.5 * (poro[1, 2:] - poro[1, :WX])
-    divergence = divergence + 0.5 * (y_next(drag[1], 0, 1) - y_previous(drag[1], 0, 1))
+    def step_y(v, low, high):
+        return jnp.where(yi == 7, high, pltpu.roll(v, 7, 1)), jnp.where(yi == 0, low, pltpu.roll(v, 1, 1))
+
+    after, before = step_y(drag[1], dy_recv[0][:, None, :], dy_recv[1][:, None, :])
+    divergence = 0.5 * (dx_face[2:] - dx_face[:WX])
+    divergence = divergence + 0.5 * (after - before)
     divergence = divergence + 0.5 * (z_next(drag[2]) - z_previous(drag[2]))
     right_side = source[...] - divergence
-    x_upper = 0.5 * (porosity + poro[0, 2:])
-    x_lower = 0.5 * (poro[0, :WX] + porosity)
-    y_upper = 0.5 * (porosity + y_next(porosity, 0, 0))
-    y_lower = 0.5 * (y_previous(porosity, 0, 0) + porosity)
-    z_upper = 0.5 * (porosity + z_next(porosity))
-    z_lower = z_previous(z_upper)
-    precond = 1.0 / (diag_shift + x_upper + x_lower + y_upper + y_lower + z_upper + z_lower)
-    for i, weights in enumerate((x_upper, x_lower, y_upper, y_lower, z_upper, z_lower, precond)):
-        face[i] = weights
-
-    def operate(k, u):
-        v = u[1 : WX + 1]
-        exchange(k, lambda x: u.at[x], tuple(v[:, y][None] for y in (7, 0)))
+    after, before = step_y(porosity, poro[own_x, 7:8], poro[own_x, 16:17])
+
+    def precondition(p, x_after, x_before, y_after, y_before):
+        x_upper, x_lower = 0.5 * (p + x_after), 0.5 * (x_before + p)
+        y_upper, y_lower = 0.5 * (p + y_after), 0.5 * (y_before + p)
+        z_upper = 0.5 * (p + z_next(p))
+        z_lower = z_previous(z_upper)
+        weights = (x_upper, x_lower, y_upper, y_lower, z_upper, z_lower)
+        return weights, 1.0 / (diag_shift + x_upper + x_lower + y_upper + y_lower + z_upper + z_lower)
+
+    start = precondition(
+        porosity, poro[pl.ds(HALO + 1, WX), own_y], poro[pl.ds(HALO - 1, WX), own_y], after, before
+    )[1] * right_side
+    u0[own_x, own_y] = start
+    more = send_halo(1, u0)
+
+    for copy in halo[4:]:
+        copy.wait()
+    place_corners(0, poro)
+
+    def y_steps(v):
+        return pltpu.roll(v, 23, 1), pltpu.roll(v, 1, 1)
+
+    p = poro[1 : WIDE - 1]
+    weights, precond = precondition(p, poro[2:], poro[: WIDE - 2], *y_steps(p))
+    for i, w in enumerate(weights + (precond,)):
+        face[i] = w
+    for copy in more:
+        copy.wait()
+    place_faces(1, u0)
+    place_corners(1, u0)
+
+    def operate(ref, low):
+        high = WIDE - low
+        v = ref[low:high]
+        w = [face[i, low - 1 : high - 1] for i in range(6)]
+        y_after, y_before = y_steps(v)
         result = diag_shift * v
-        result = result + face[0] * (v - u[2:])
-        result = result + face[1] * (v - u[:WX])
-        result = result + face[2] * (v - y_next(v, k, 0))
-        result = result + face[3] * (v - y_previous(v, k, 0))
-        result = result + face[4] * (v - z_next(v))
-        result = result + face[5] * (v - z_previous(v))
-        return v, result
+        result = result + w[0] * (v - ref[low + 1 : high + 1])
+        result = result + w[1] * (v - ref[low - 1 : high - 1])
+        result = result + w[2] * (v - y_after)
+        result = result + w[3] * (v - y_before)
+        result = result + w[4] * (v - z_next(v))
+        return result + w[5] * (v - z_previous(v))
 
     def partial_sum(a, b):
         product = jnp.sum(a * b, 0)
         return jnp.sum(product[:, :128] + product[:, 128:], 0, keepdims=True)
 
-    start = precond * right_side
-    u0[1 : WX + 1] = start
-    moments = [partial_sum(right_side, start)]
-    v0, a0 = operate(1, u0)
-    v1 = face[6] * a0
-    u1[1 : WX + 1] = v1
-    moments += [partial_sum(v0, a0), partial_sum(v1, a0)]
-    v1, a1 = operate(2, u1)
-    v2 = face[6] * a1
-    u2[1 : WX + 1] = v2
-    moments += [partial_sum(v1, a1), partial_sum(v2, a1)]
-    v2, a2 = operate(3, u2)
-    moments += [partial_sum(v2, a2)]
+    a0 = operate(u0, 1)
+    u1[1 : WIDE - 1] = face[6] * a0
+    a1 = operate(u1, 2)
+    u2[2 : WIDE - 2] = face[6, 1 : WX + 3] * a1
+    a2 = operate(u2, 3)[:, 8:16]
+    a0, a1 = a0[2 : WX + 2, 8:16], a1[1 : WX + 1, 8:16]
+    v1, v2 = u1[own_x, own_y], u2[own_x, own_y]
+    moments = [
+        partial_sum(right_side, start),
+        partial_sum(start, a0),
+        partial_sum(v1, a0),
+        partial_sum(v1, a1),
+        partial_sum(v2, a1),
+        partial_sum(v2, a2),
+    ]
 
     zero = jnp.zeros((2, 128), f32)
     mine = jnp.concatenate(moments + [zero], 0)
@@ -271,13 +338,13 @@
     c1 = r1 / d2 - l32 * c2
     c0 = m0 / m1 - l21 * c1 - l31 * c2
     c0, c1, c2 = [c.reshape(1, 1, 1) for c in (c0, c1, c2)]
-    pressure_out[...] = c0 * u0[1 : WX + 1] + c1 * u1[1 : WX + 1] + c2 * u2[1 : WX + 1]
+    pressure_out[...] = c0 * u0[own_x, own_y] + c1 * u1[own_x, own_y] + c2 * u2[own_x, own_y]
 
 
 def run(counts, columns, layers, data, source):
     vmem = pl.BlockSpec(memory_space=pltpu.VMEM)
     block = (WX, WY, NZ)
-    padded = (WX + 2, WY, NZ)
+    wide = (WIDE, 24, NZ)
     dma = pltpu.SemaphoreType.DMA
     return pl.pallas_call(
         kernel,
@@ -296,17 +363,21 @@
             pltpu.VMEM((32, NZ), f32),
             pltpu.VMEM((64, NZ), f32),
             pltpu.VMEM((8, NZ), f32),
-            pltpu.VMEM((2,) + padded, f32),
-            pltpu.VMEM((7,) + block, f32),
-            pltpu.VMEM((4, 2, 2, WX, NZ), f32),
-            pltpu.VMEM((4, 2, 2, WX, NZ), f32),
-            pltpu.VMEM(padded, f32),
-            pltpu.VMEM(padded, f32),
-            pltpu.VMEM(padded, f32),
+            pltpu.VMEM((WX + 2, WY, NZ), f32),
+            pltpu.VMEM((2, WX, NZ), f32),
+            pltpu.VMEM((2, WX, NZ), f32),
+            pltpu.VMEM((2, 2, WX // 2, 8, NZ), f32),
+            pltpu.VMEM((2, 2, WX // 2, 8, NZ), f32),
+            pltpu.VMEM((2, 4, 8, NZ), f32),
+            pltpu.VMEM((7, WIDE - 2, 24, NZ), f32),
+            pltpu.VMEM(wide, f32),
+            pltpu.VMEM(wide, f32),
+            pltpu.VMEM(wide, f32),
+            pltpu.VMEM(wide, f32),
             pltpu.VMEM((2, 8, 128), f32),
             pltpu.VMEM((NGX, 8, 128), f32),
             pltpu.VMEM((NGY, 8, 128), f32),
-            dma((3,)), dma((3,)), dma((4, 4)), dma((4, 4)),
+            dma((3,)), dma((3,)), dma((4,)), dma((4,)), dma((2, 8)), dma((2, 8)),
             dma((NGX,)), dma((NGX,)), dma((NGY,)), dma((NGY,)),
         ],
         compiler_params=pltpu.CompilerParams(

time: 95 us -> 82.1 us (0.86)
  Pallas kernels: 89.7 us -> 76.8 us
    pallas_call x1, Pallas kernels: 89.7 us -> 76.8 us  [run(): pl.pallas_call(kernel, out_shape=(jax.ShapeDtypeStruct(block, f32), jax.S...]
where the time goes in v4:
time: 82.1 us; the launch traced here: 82 us
  Pallas kernels  76.8 us (94%)
  local copies, waits for them, and re-layouts  4.46 us (5%)
    pallas_call x1, Pallas kernels, run(): pl.pallas_call(kernel, out_shape=(jax.ShapeDtypeStruct(block, f32), jax.S...  76.8 us
    unnamed x12, local copies, waits for them, and re-layouts  4.46 us

profile of v4, /device:TPU:1, one launch (start us, length us, event | category | flops | bytes accessed | tf_op | source)
XLA Modules:
  0.0 82.0 jit_solution(5551714814477165794)
XLA Ops:
  0.6 0.0 copy-start
  0.6 0.0 copy-start.1
  0.7 0.0 copy-start.2
  0.7 1.8 %copy.10 = f32[1,128,7,256]{3,2,1,0:T(8,128)S(1)} copy(f32[1,128,7,256]{3,1,2,0:T(8,128)} %param.8) | data formatting | bytes 1835008 | tf_op args[3]
  2.4 0.0 copy-start.3
  2.4 0.0 copy-done
  2.5 0.0 copy-done.1
  2.5 0.0 copy-done.2
  2.5 0.6 copy-done.3
  3.1 76.8 %coupling.1 = (f32[16,8,256]{2,1,0:T(8,128)S(1)}, f32[3,16,8,256]{3,2,1,0:T(8,128)S(1)}, f32[16,8,256]{2,1,0:T(8,128)S(1)}) custom-call(s32[1,128]{1,0:T(1,128)S(1)} %copy-done.3, s32[128,256]{1,0:T(8,128)S(1)} %bitcast.6, s32[128,256]{1,0:T(8,128)S(1)} %bitcast.7, f32[128,7,256]{2,1,0:T(8,128)S(1)} %bitcast.5, f32[16,8,256]{2,1,0:T(8,128)S(1)} %copy-done.2), custom_call_target="tpu_custom_call" | custom-call | tf_op jit(solution)/shard_map/coupling/pallas_call | solution.py:349
  79.9 0.7 copy.14
  80.6 0.7 copy.15
  81.3 0.7 copy.16
Async XLA Ops:
  0.6 1.8 %copy-start = (s32[1,128,256]{2,1,0:T(8,128)S(1)}, s32[1,128,256]{2,1,0:T(8,128)}, u32[]{:S(2)}) copy-start(s32[1,128,256]{2,1,0:T(8,128)} %param.5) | copy-start | bytes 393220
  0.6 1.8 %copy-start.1 = (s32[1,128,256]{2,1,0:T(8,128)S(1)}, s32[1,128,256]{2,1,0:T(8,128)}, u32[]{:S(2)}) copy-start(s32[1,128,256]{2,1,0:T(8,128)} %param.6) | copy-start | bytes 393220
  0.7 1.8 %copy-start.2 = (f32[16,8,256]{2,1,0:T(8,128)S(1)}, f32[16,8,256]{2,1,0:T(8,128)}, u32[]{:S(2)}) copy-start(f32[16,8,256]{2,1,0:T(8,128)} %source.1) | copy-start | bytes 393220
  2.4 0.7 copy-start.3

commit v5 on v4

--- a/solution.py
+++ b/solution.py
@@ -57,7 +57,7 @@
 
 def kernel(
     counts, columns, layers, data, source, porosity_out, drag_out, pressure_out,
-    packed, slots, total, all_send, all_recv,
+    packed, slots, total, ready, all_send, all_recv,
     over_x, over_y, over_c, dx_face, dy_send, dy_recv, y_send, y_recv, corner, face, poro, u0, u1, u2,
     red, red_x, red_y, over_send, over_recv, dx_send, dx_recv, halo_send, halo_recv, rx_send, rx_recv, ry_send, ry_recv,
 ):
@@ -65,10 +65,18 @@
     xp, xm = lax.rem(gx + 1, NGX), lax.rem(gx + NGX - 1, NGX)
     yp, ym = lax.rem(gy + 1, NGY), lax.rem(gy + NGY - 1, NGY)
 
+    near = NGX + NGY - 1
+
     def peer(k):
-        return lax.rem(gx + lax.rem(k, NGX), NGX), lax.rem(gy + lax.div(k, NGX), NGY)
+        if isinstance(k, int) and k < near:
+            step_x, step_y = (k, 0) if k < NGX else (0, k - NGX + 1)
+        else:
+            step_x, step_y = 1 + lax.rem(k - near, NGX - 1), 1 + lax.div(k - near, NGX - 1)
+        return lax.rem(gx + step_x, NGX), lax.rem(gy + step_y, NGY)
 
     barrier = pltpu.get_barrier_semaphore()
+    for k in range(1, near):
+        pl.semaphore_signal(barrier, inc=1, device_id=peer(k), device_id_type=MESH)
 
     lane = lax.broadcasted_iota(jnp.int32, (1, CAP), 1)
 
@@ -81,22 +89,13 @@
         target[k, :, CAP * 7 : CAP * 8] = columns[pl.ds(d, 1)].astype(f32)
         target[k, :, CAP * 8 :] = layers[pl.ds(d, 1)].astype(f32)
 
-    def greet(k, carry):
-        pl.semaphore_signal(barrier, inc=1, device_id=peer(k), device_id_type=MESH)
-        return carry
-
-    def pack_one(k, carry):
+    def pack_one(k):
         px, py = peer(k)
         pack(packed, k, px * NGY + py)
-        return carry
-
-    def greet_and_pack(k, carry):
-        return pack_one(k, greet(k, carry))
-
-    lax.fori_loop(1, AHEAD * GROUP, greet_and_pack, 0)
-    lax.fori_loop(AHEAD * GROUP, DEVICES, greet, 0)
+
+    for k in range(1, near):
+        pack_one(k)
     pack(slots, 0, gx * NGY + gy)
-    pl.semaphore_wait(barrier, DEVICES - 1)
 
     def ship(group, g):
         k = group * GROUP + g
@@ -109,10 +108,16 @@
             device_id_type=MESH,
         ).start()
 
-    for group in range(AHEAD):
-        for g in range(GROUP):
-            if group + g > 0:
-                ship(group, g)
+    pl.semaphore_wait(barrier, near - 1)
+    for k in range(1, NGY):
+        pl.semaphore_signal(ready, inc=1, device_id=(gx, lax.rem(gy + k, NGY)), device_id_type=MESH)
+    for k in range(1, near):
+        ship(k // GROUP, k % GROUP)
+    for k in range(near, AHEAD * GROUP):
+        pack_one(k)
+    pl.semaphore_wait(ready, NGY - 1)
+    for k in range(near, AHEAD * GROUP):
+        ship(k // GROUP, k % GROUP)
 
     def arrived(group, first, count):
         block = slots.at[pl.ds(first, count)]
@@ -139,7 +144,7 @@
 
         if shipping:
             for g in range(GROUP):
-                pack_one((i + AHEAD) * GROUP + g, 0)
+                pack_one((i + AHEAD) * GROUP + g)
                 ship(i + AHEAD, g)
         total[...] += add_group(i)
 
@@ -332,10 +337,10 @@
     e32 = m4 - l31 * m2
     r1 = m1 - l21 * m0
     r2 = m2 - l31 * m0
-    l32 = e32 / d2
+    l32 = jnp.where(d2 > 1e-8 * m3, e32 / d2, 0.0)
     d3 = (m5 - l31 * m3) - l32 * e32
-    c2 = (r2 - l32 * r1) / d3
-    c1 = r1 / d2 - l32 * c2
+    c2 = jnp.where(d3 > 1e-8 * m5, (r2 - l32 * r1) / d3, 0.0)
+    c1 = jnp.where(d2 > 1e-8 * m3, r1 / d2 - l32 * c2, 0.0)
     c0 = m0 / m1 - l21 * c1 - l31 * c2
     c0, c1, c2 = [c.reshape(1, 1, 1) for c in (c0, c1, c2)]
     pressure_out[...] = c0 * u0[own_x, own_y] + c1 * u1[own_x, own_y] + c2 * u2[own_x, own_y]
@@ -359,7 +364,7 @@
             pltpu.VMEM((DEVICES, 1, VALUES * CAP), f32),
             pltpu.VMEM((DEVICES, 1, VALUES * CAP), f32),
             pltpu.VMEM((ROWS, NZ), f32),
-            dma(()), dma((DEVICES // GROUP,)),
+            pltpu.SemaphoreType.REGULAR, dma(()), dma((DEVICES // GROUP,)),
             pltpu.VMEM((32, NZ), f32),
             pltpu.VMEM((64, NZ), f32),
             pltpu.VMEM((8, NZ), f32),

time: 82.1 us -> 79.1 us (0.963)
  Pallas kernels: 76.8 us -> 73.8 us
    pallas_call x1, Pallas kernels: 76.8 us -> 73.8 us  [run(): pl.pallas_call(kernel, out_shape=(jax.ShapeDtypeStruct(block, f32), jax.S...]
where the time goes in v5:
time: 79.1 us; the launch traced here: 79 us
  Pallas kernels  73.8 us (93%)
  local copies, waits for them, and re-layouts  4.46 us (6%)
    pallas_call x1, Pallas kernels, run(): pl.pallas_call(kernel, out_shape=(jax.ShapeDtypeStruct(block, f32), jax.S...  73.8 us
    unnamed x12, local copies, waits for them, and re-layouts  4.46 us

profile of v5, /device:TPU:1, one launch (start us, length us, event | category | flops | bytes accessed | tf_op | source)
XLA Modules:
  0.0 79.0 jit_solution(14233810272469293255)
XLA Ops:
  0.6 0.0 copy-start
  0.6 0.0 copy-start.1
  0.7 0.0 copy-start.2
  0.7 1.8 %copy.10 = f32[1,128,7,256]{3,2,1,0:T(8,128)S(1)} copy(f32[1,128,7,256]{3,1,2,0:T(8,128)} %param.8) | data formatting | bytes 1835008 | tf_op args[3]
  2.4 0.0 copy-start.3
  2.4 0.0 copy-done
  2.5 0.0 copy-done.1
  2.5 0.0 copy-done.2
  2.5 0.6 copy-done.3
  3.1 73.8 %coupling.1 = (f32[16,8,256]{2,1,0:T(8,128)S(1)}, f32[3,16,8,256]{3,2,1,0:T(8,128)S(1)}, f32[16,8,256]{2,1,0:T(8,128)S(1)}) custom-call(s32[1,128]{1,0:T(1,128)S(1)} %copy-done.3, s32[128,256]{1,0:T(8,128)S(1)} %bitcast.6, s32[128,256]{1,0:T(8,128)S(1)} %bitcast.7, f32[128,7,256]{2,1,0:T(8,128)S(1)} %bitcast.5, f32[16,8,256]{2,1,0:T(8,128)S(1)} %copy-done.2), custom_call_target="tpu_custom_call" | custom-call | tf_op jit(solution)/shard_map/coupling/pallas_call | solution.py:354
  76.9 0.7 copy.14
  77.6 0.7 copy.15
  78.3 0.7 copy.16
Async XLA Ops:
  0.6 1.8 %copy-start = (s32[1,128,256]{2,1,0:T(8,128)S(1)}, s32[1,128,256]{2,1,0:T(8,128)}, u32[]{:S(2)}) copy-start(s32[1,128,256]{2,1,0:T(8,128)} %param.5) | copy-start | bytes 393220
  0.6 1.8 %copy-start.1 = (s32[1,128,256]{2,1,0:T(8,128)S(1)}, s32[1,128,256]{2,1,0:T(8,128)}, u32[]{:S(2)}) copy-start(s32[1,128,256]{2,1,0:T(8,128)} %param.6) | copy-start | bytes 393220
  0.7 1.8 %copy-start.2 = (f32[16,8,256]{2,1,0:T(8,128)S(1)}, f32[16,8,256]{2,1,0:T(8,128)}, u32[]{:S(2)}) copy-start(f32[16,8,256]{2,1,0:T(8,128)} %source.1) | copy-start | bytes 393220
  2.4 0.7 copy-start.3

commit v6 on v5

--- a/solution.py
+++ b/solution.py
@@ -58,8 +58,8 @@
 def kernel(
     counts, columns, layers, data, source, porosity_out, drag_out, pressure_out,
     packed, slots, total, ready, all_send, all_recv,
-    over_x, over_y, over_c, dx_face, dy_send, dy_recv, y_send, y_recv, corner, face, poro, u0, u1, u2,
-    red, red_x, red_y, over_send, over_recv, dx_send, dx_recv, halo_send, halo_recv, rx_send, rx_recv, ry_send, ry_recv,
+    over_x, over_y, over_c, next_x, diag_y, diag_x, cross_y, cross_x, tip, f_send, f_recv, y_send, y_recv, corner, face, poro, u0, u1, u2,
+    red, red_x, red_y, edge_send, edge_recv, halo_send, halo_recv, rx_send, rx_recv, ry_send, ry_recv,
 ):
     gx, gy = lax.axis_index("gx"), lax.axis_index("gy")
     xp, xm = lax.rem(gx + 1, NGX), lax.rem(gx + NGX - 1, NGX)
@@ -161,17 +161,33 @@
         copy.start()
         return copy
 
-    copies = [
-        send(total.at[pl.ds(512, 32)], over_x, over_send.at[0], over_recv.at[0], (xp, gy)),
-        send(total.at[pl.ds(MAIN, 64)], over_y, over_send.at[1], over_recv.at[1], (gx, yp)),
-        send(total.at[pl.ds(MAIN + 64, 8)], over_c, over_send.at[2], over_recv.at[2], (xp, yp)),
+    top, side = 4 * WX * WY, 4 * WX
+    ends = total[top:MAIN].reshape(4, 8, NZ)
+    tip[...] = jnp.concatenate([ends[:, 7], ends[:, 0]], 0)
+    blocks = total[:top].reshape(WX, 4, 8, NZ)
+    for i, y in enumerate((7, 0)):
+        f_send[i, 0] = blocks[:, 0, y]
+        f_send[i, 1] = blocks[:, 2, y]
+    routes = [
+        (total.at[pl.ds(MAIN + side - 8, 16)], diag_y, (xp, yp)),
+        (tip, diag_x, (xp, yp)),
+        (total.at[pl.ds(MAIN, 8)], cross_y, (xm, yp)),
+        (tip, cross_x, (xp, ym)),
+        (total.at[pl.ds(MAIN, side + 8)], over_y, (gx, yp)),
+        (f_send.at[0], f_recv.at[0], (gx, yp)),
+        (f_send.at[1], f_recv.at[1], (gx, ym)),
+        (total.at[pl.ds(top - 32, 64)], over_x, (xp, gy)),
+        (total.at[pl.ds(MAIN + side, 8)], over_c, (xp, gy)),
+        (total.at[pl.ds(0, 16)], next_x, (xm, gy)),
     ]
-    for copy in copies:
+    edges = [send(src, dst, edge_send.at[i], edge_recv.at[i], to) for i, (src, dst, to) in enumerate(routes)]
+    for copy in edges:
         copy.wait()
-    from_y = jnp.concatenate([over_y[:8] + over_c[...], over_y[8:]], 0)
-    inner = total[:512].reshape(64, 8, NZ)
-    inner = jnp.concatenate([inner[:4] + over_x[...].reshape(4, 8, NZ), inner[4:]], 0)
-    row = lax.broadcasted_iota(jnp.int32, (64, 8, NZ), 1)
+
+    from_y = jnp.concatenate([over_y[:8] + diag_y[8:], over_y[8:side]], 0)
+    inner = total[:top].reshape(side, 8, NZ)
+    inner = jnp.concatenate([inner[:4] + over_x[32:].reshape(4, 8, NZ), inner[4:]], 0)
+    row = lax.broadcasted_iota(jnp.int32, (side, 8, NZ), 1)
     inner = inner + jnp.where(row == 0, from_y[:, None, :], 0.0)
     inner = inner.reshape(WX, 4, 8, NZ)
     porosity = 1.0 / (1.0 + inner[:, 0])
@@ -194,14 +210,14 @@
             return send(src, dst, halo_send.at[k, i], halo_recv.at[k, i], to)
 
         return [
-            put(0, y_send.at[k, 0], y_recv.at[k, 0], (gx, yp)),
-            put(1, y_send.at[k, 1], y_recv.at[k, 1], (gx, ym)),
-            put(2, ref.at[pl.ds(WX, HALO), own_y], ref.at[pl.ds(0, HALO), own_y], (xp, gy)),
-            put(3, ref.at[pl.ds(HALO, HALO), own_y], ref.at[pl.ds(WX + HALO, HALO), own_y], (xm, gy)),
-            put(4, y_send.at[k, 0, last], corner.at[k, 0], (xp, yp)),
-            put(5, y_send.at[k, 1, last], corner.at[k, 1], (xp, ym)),
-            put(6, y_send.at[k, 0, 0], corner.at[k, 2], (xm, yp)),
-            put(7, y_send.at[k, 1, 0], corner.at[k, 3], (xm, ym)),
+            put(0, y_send.at[k, 0, last], corner.at[k, 0], (xp, yp)),
+            put(1, y_send.at[k, 1, last], corner.at[k, 1], (xp, ym)),
+            put(2, y_send.at[k, 0, 0], corner.at[k, 2], (xm, yp)),
+            put(3, y_send.at[k, 1, 0], corner.at[k, 3], (xm, ym)),
+            put(4, y_send.at[k, 0], y_recv.at[k, 0], (gx, yp)),
+            put(5, y_send.at[k, 1], y_recv.at[k, 1], (gx, ym)),
+            put(6, ref.at[pl.ds(WX, HALO), own_y], ref.at[pl.ds(0, HALO), own_y], (xp, gy)),
+            put(7, ref.at[pl.ds(HALO, HALO), own_y], ref.at[pl.ds(WX + HALO, HALO), own_y], (xm, gy)),
         ]
 
     def place_faces(k, ref):
@@ -218,19 +234,19 @@
             ref[x + 1, 16:] = pltpu.roll(high, 4, 0)
 
     poro[own_x, own_y] = porosity
-    dx_face[1 : WX + 1] = drag[0]
-    dy_send[0] = drag[1][:, 7]
-    dy_send[1] = drag[1][:, 0]
-    drags = [
-        send(dy_send.at[0], dy_recv.at[0], dx_send.at[0], dx_recv.at[0], (gx, yp)),
-        send(dy_send.at[1], dy_recv.at[1], dx_send.at[1], dx_recv.at[1], (gx, ym)),
-        send(dx_face.at[WX], dx_face.at[0], dx_send.at[2], dx_recv.at[2], (xp, gy)),
-        send(dx_face.at[1], dx_face.at[WX + 1], dx_send.at[3], dx_recv.at[3], (xm, gy)),
-    ]
     halo = send_halo(0, poro)
-    for copy in drags + halo[:4]:
-        copy.wait()
-    place_faces(0, poro)
+
+    first_y = lax.broadcasted_iota(jnp.int32, (2, 8, NZ), 1) == 0
+    below_x = over_x[:16].reshape(2, 8, NZ) + jnp.where(first_y, diag_y[4:6][:, None, :], 0.0)
+    above_x = next_x[...].reshape(2, 8, NZ) + total[top : top + 16].reshape(2, 8, NZ)
+    above_x = above_x + jnp.where(first_y, (cross_y[:2] + over_y[side : side + 2])[:, None, :], 0.0)
+    first_x = lax.broadcasted_iota(jnp.int32, (WX, NZ), 0) == 0
+    mine = total[MAIN : MAIN + side].reshape(WX, 4, NZ)
+    below_y, above_y = [], []
+    for i, f in enumerate((0, 2)):
+        below_y.append(f_recv[0, i] + jnp.where(first_x, diag_x[f : f + 1], 0.0))
+        corner_sum = cross_x[4 + f : 5 + f] + over_c[f : f + 1]
+        above_y.append(f_recv[1, i] + mine[:, f] + jnp.where(first_x, corner_sum, 0.0))
 
     yi = lax.broadcasted_iota(jnp.int32, (WX, 8, NZ), 1)
 
@@ -243,12 +259,18 @@
     def step_y(v, low, high):
         return jnp.where(yi == 7, high, pltpu.roll(v, 7, 1)), jnp.where(yi == 0, low, pltpu.roll(v, 1, 1))
 
-    after, before = step_y(drag[1], dy_recv[0][:, None, :], dy_recv[1][:, None, :])
-    divergence = 0.5 * (dx_face[2:] - dx_face[:WX])
+    def step_x(v, low, high):
+        return jnp.concatenate([v[1:], high[None]], 0), jnp.concatenate([low[None], v[: WX - 1]], 0)
+
+    after, before = step_y(drag[1], below_y[1][:, None, :], above_y[1][:, None, :])
+    x_after, x_before = step_x(drag[0], below_x[1], above_x[1])
+    divergence = 0.5 * (x_after - x_before)
     divergence = divergence + 0.5 * (after - before)
     divergence = divergence + 0.5 * (z_next(drag[2]) - z_previous(drag[2]))
     right_side = source[...] - divergence
-    after, before = step_y(porosity, poro[own_x, 7:8], poro[own_x, 16:17])
+    low, high = 1.0 / (1.0 + below_y[0]), 1.0 / (1.0 + above_y[0])
+    after, before = step_y(porosity, low[:, None, :], high[:, None, :])
+    x_after, x_before = step_x(porosity, 1.0 / (1.0 + below_x[0]), 1.0 / (1.0 + above_x[0]))
 
     def precondition(p, x_after, x_before, y_after, y_before):
         x_upper, x_lower = 0.5 * (p + x_after), 0.5 * (x_before + p)
@@ -258,14 +280,13 @@
         weights = (x_upper, x_lower, y_upper, y_lower, z_upper, z_lower)
         return weights, 1.0 / (diag_shift + x_upper + x_lower + y_upper + y_lower + z_upper + z_lower)
 
-    start = precondition(
-        porosity, poro[pl.ds(HALO + 1, WX), own_y], poro[pl.ds(HALO - 1, WX), own_y], after, before
-    )[1] * right_side
+    start = precondition(porosity, x_after, x_before, after, before)[1] * right_side
     u0[own_x, own_y] = start
     more = send_halo(1, u0)
 
-    for copy in halo[4:]:
+    for copy in halo:
         copy.wait()
+    place_faces(0, poro)
     place_corners(0, poro)
 
     def y_steps(v):
@@ -365,12 +386,17 @@
             pltpu.VMEM((DEVICES, 1, VALUES * CAP), f32),
             pltpu.VMEM((ROWS, NZ), f32),
             pltpu.SemaphoreType.REGULAR, dma(()), dma((DEVICES // GROUP,)),
-            pltpu.VMEM((32, NZ), f32),
             pltpu.VMEM((64, NZ), f32),
+            pltpu.VMEM((72, NZ), f32),
             pltpu.VMEM((8, NZ), f32),
-            pltpu.VMEM((WX + 2, WY, NZ), f32),
-            pltpu.VMEM((2, WX, NZ), f32),
-            pltpu.VMEM((2, WX, NZ), f32),
+            pltpu.VMEM((16, NZ), f32),
+            pltpu.VMEM((16, NZ), f32),
+            pltpu.VMEM((8, NZ), f32),
+            pltpu.VMEM((8, NZ), f32),
+            pltpu.VMEM((8, NZ), f32),
+            pltpu.VMEM((8, NZ), f32),
+            pltpu.VMEM((2, 2, WX, NZ), f32),
+            pltpu.VMEM((2, 2, WX, NZ), f32),
             pltpu.VMEM((2, 2, WX // 2, 8, NZ), f32),
             pltpu.VMEM((2, 2, WX // 2, 8, NZ), f32),
             pltpu.VMEM((2, 4, 8, NZ), f32),
@@ -382,7 +408,7 @@
             pltpu.VMEM((2, 8, 128), f32),
             pltpu.VMEM((NGX, 8, 128), f32),
             pltpu.VMEM((NGY, 8, 128), f32),
-            dma((3,)), dma((3,)), dma((4,)), dma((4,)), dma((2, 8)), dma((2, 8)),
+            dma((10,)), dma((10,)), dma((2, 8)), dma((2, 8)),
             dma((NGX,)), dma((NGX,)), dma((NGY,)), dma((NGY,)),
         ],
         compiler_params=pltpu.CompilerParams(

time: 79.1 us -> 77 us (0.973)
  Pallas kernels: 73.8 us -> 71.7 us
    pallas_call x1, Pallas kernels: 73.8 us -> 71.7 us  [run(): pl.pallas_call(kernel, out_shape=(jax.ShapeDtypeStruct(block, f32), jax.S...]
where the time goes in v6:
time: 77 us; the launch traced here: 76.8 us
  Pallas kernels  71.7 us (93%)
  local copies, waits for them, and re-layouts  4.46 us (6%)
    pallas_call x1, Pallas kernels, run(): pl.pallas_call(kernel, out_shape=(jax.ShapeDtypeStruct(block, f32), jax.S...  71.7 us
    unnamed x12, local copies, waits for them, and re-layouts  4.46 us

profile of v6, /device:TPU:1, one launch (start us, length us, event | category | flops | bytes accessed | tf_op | source)
XLA Modules:
  0.0 76.8 jit_solution(10429300603668992166)
XLA Ops:
  0.6 0.0 copy-start
  0.6 0.0 copy-start.1
  0.7 0.0 copy-start.2
  0.7 1.8 %copy.10 = f32[1,128,7,256]{3,2,1,0:T(8,128)S(1)} copy(f32[1,128,7,256]{3,1,2,0:T(8,128)} %param.8) | data formatting | bytes 1835008 | tf_op args[3]
  2.4 0.0 copy-start.3
  2.4 0.0 copy-done
  2.5 0.0 copy-done.1
  2.5 0.0 copy-done.2
  2.5 0.6 copy-done.3
  3.1 71.7 %coupling.1 = (f32[16,8,256]{2,1,0:T(8,128)S(1)}, f32[3,16,8,256]{3,2,1,0:T(8,128)S(1)}, f32[16,8,256]{2,1,0:T(8,128)S(1)}) custom-call(s32[1,128]{1,0:T(1,128)S(1)} %copy-done.3, s32[128,256]{1,0:T(8,128)S(1)} %bitcast.6, s32[128,256]{1,0:T(8,128)S(1)} %bitcast.7, f32[128,7,256]{2,1,0:T(8,128)S(1)} %bitcast.5, f32[16,8,256]{2,1,0:T(8,128)S(1)} %copy-done.2), custom_call_target="tpu_custom_call" | custom-call | tf_op jit(solution)/shard_map/coupling/pallas_call | solution.py:375
  74.8 0.7 copy.14
  75.4 0.7 copy.15
  76.2 0.7 copy.16
Async XLA Ops:
  0.6 1.8 %copy-start = (s32[1,128,256]{2,1,0:T(8,128)S(1)}, s32[1,128,256]{2,1,0:T(8,128)}, u32[]{:S(2)}) copy-start(s32[1,128,256]{2,1,0:T(8,128)} %param.5) | copy-start | bytes 393220
  0.6 1.8 %copy-start.1 = (s32[1,128,256]{2,1,0:T(8,128)S(1)}, s32[1,128,256]{2,1,0:T(8,128)}, u32[]{:S(2)}) copy-start(s32[1,128,256]{2,1,0:T(8,128)} %param.6) | copy-start | bytes 393220
  0.7 1.8 %copy-start.2 = (f32[16,8,256]{2,1,0:T(8,128)S(1)}, f32[16,8,256]{2,1,0:T(8,128)}, u32[]{:S(2)}) copy-start(f32[16,8,256]{2,1,0:T(8,128)} %source.1) | copy-start | bytes 393220
  2.4 0.7 copy-start.3

commit v7 on v6

--- a/solution.py
+++ b/solution.py
@@ -322,9 +322,18 @@
     u1[1 : WIDE - 1] = face[6] * a0
     a1 = operate(u1, 2)
     u2[2 : WIDE - 2] = face[6, 1 : WX + 3] * a1
-    a2 = operate(u2, 3)[:, 8:16]
+    v2 = u2[own_x, own_y]
+    w = [face[i, HALO - 1 : HALO - 1 + WX, 8:16] for i in range(6)]
+    y_after, y_before = step_y(v2, u2[own_x, 7:8], u2[own_x, 16:17])
+    a2 = diag_shift * v2
+    a2 = a2 + w[0] * (v2 - u2[pl.ds(HALO + 1, WX), own_y])
+    a2 = a2 + w[1] * (v2 - u2[pl.ds(HALO - 1, WX), own_y])
+    a2 = a2 + w[2] * (v2 - y_after)
+    a2 = a2 + w[3] * (v2 - y_before)
+    a2 = a2 + w[4] * (v2 - z_next(v2))
+    a2 = a2 + w[5] * (v2 - z_previous(v2))
     a0, a1 = a0[2 : WX + 2, 8:16], a1[1 : WX + 1, 8:16]
-    v1, v2 = u1[own_x, own_y], u2[own_x, own_y]
+    v1 = u1[own_x, own_y]
     moments = [
         partial_sum(right_side, start),
         partial_sum(start, a0),

time: 77 us -> 77 us (level)
  no operation moved by 1% of the time
where the time goes in v7:
time: 77 us; the launch traced here: 76.9 us
  Pallas kernels  71.7 us (93%)
  local copies, waits for them, and re-layouts  4.46 us (6%)
    pallas_call x1, Pallas kernels, run(): pl.pallas_call(kernel, out_shape=(jax.ShapeDtypeStruct(block, f32), jax.S...  71.7 us
    unnamed x12, local copies, waits for them, and re-layouts  4.46 us

profile of v7, /device:TPU:1, one launch (start us, length us, event | category | flops | bytes accessed | tf_op | source)
XLA Modules:
  0.0 76.9 jit_solution(11709207282171151812)
XLA Ops:
  0.6 0.0 copy-start
  0.6 0.0 copy-start.1
  0.7 0.0 copy-start.2
  0.7 1.8 %copy.10 = f32[1,128,7,256]{3,2,1,0:T(8,128)S(1)} copy(f32[1,128,7,256]{3,1,2,0:T(8,128)} %param.8) | data formatting | bytes 1835008 | tf_op args[3]
  2.4 0.0 copy-start.3
  2.4 0.0 copy-done
  2.5 0.0 copy-done.1
  2.5 0.0 copy-done.2
  2.5 0.6 copy-done.3
  3.1 71.7 %coupling.1 = (f32[16,8,256]{2,1,0:T(8,128)S(1)}, f32[3,16,8,256]{3,2,1,0:T(8,128)S(1)}, f32[16,8,256]{2,1,0:T(8,128)S(1)}) custom-call(s32[1,128]{1,0:T(1,128)S(1)} %copy-done.3, s32[128,256]{1,0:T(8,128)S(1)} %bitcast.6, s32[128,256]{1,0:T(8,128)S(1)} %bitcast.7, f32[128,7,256]{2,1,0:T(8,128)S(1)} %bitcast.5, f32[16,8,256]{2,1,0:T(8,128)S(1)} %copy-done.2), custom_call_target="tpu_custom_call" | custom-call | tf_op jit(solution)/shard_map/coupling/pallas_call | solution.py:384
  74.8 0.7 copy.14
  75.5 0.7 copy.15
  76.2 0.7 copy.16
Async XLA Ops:
  0.6 1.8 %copy-start = (s32[1,128,256]{2,1,0:T(8,128)S(1)}, s32[1,128,256]{2,1,0:T(8,128)}, u32[]{:S(2)}) copy-start(s32[1,128,256]{2,1,0:T(8,128)} %param.5) | copy-start | bytes 393220
  0.6 1.8 %copy-start.1 = (s32[1,128,256]{2,1,0:T(8,128)S(1)}, s32[1,128,256]{2,1,0:T(8,128)}, u32[]{:S(2)}) copy-start(s32[1,128,256]{2,1,0:T(8,128)} %param.6) | copy-start | bytes 393220
  0.7 1.8 %copy-start.2 = (f32[16,8,256]{2,1,0:T(8,128)S(1)}, f32[16,8,256]{2,1,0:T(8,128)}, u32[]{:S(2)}) copy-start(f32[16,8,256]{2,1,0:T(8,128)} %source.1) | copy-start | bytes 393220
  2.4 0.7 copy-start.3
